TPU v7x, 256 devices: a whole 4x4x8 slice. The times are simulated.
256 devices in a mesh: segment: 8 (over y, x_hi), lon: 32 (over x_lo, z, core).
Axes of the slice: x: 4 (x_hi: 2, x_lo: 2; x = x_hi * 2 + x_lo), y: 4, z: 8, core: 2. Of those that a mesh axis runs over, the one named last changes fastest.
Arguments:
- fields: bfloat16 [4, 2, 12, 384, 192], P(None, None, None, 'lon'), may hold values from -6 to 6
- entry_order: int32 [4], replicated, may hold values from 0 to 3, each once
- shift_offsets: int32 [4, 2, 8], P(None, None, 'segment'), may hold values from 1 to 11
- qkv_weight: bfloat16 [2, 8, 192, 576], P(None, 'segment'), may hold values from -0.4375 to 0.4375
- out_weight: bfloat16 [2, 8, 192, 192], P(None, 'segment'), may hold values from -0.4375 to 0.4375
- up_weight: bfloat16 [2, 8, 192, 768], P(None, 'segment'), may hold values from -0.4375 to 0.4375
- down_weight: bfloat16 [2, 8, 768, 192], P(None, 'segment'), may hold values from -0.21875 to 0.21875
- attn_bias: float32 [2, 8, 2, 6, 144, 144], P(None, 'segment'), as said below
- norm_gain: float32 [2, 8, 2, 192], P(None, 'segment'), may hold values from 0.5 to 1.5
Outputs:
- result: bfloat16 [4, 2, 12, 384, 192], P(None, None, None, 'lon', 'segment')
Inputs may be any that keep to these rules, and one draw needn't show every extreme that they name: `attn_bias`: entries are at least -6.
All inputs are finite; a program needn't handle non-finite values.
Results may differ from a plain program's by a relative error of at most 0.022.
Values may be sent and summed in bfloat16 or wider, within the bound.
A program may use at most 64 MiB of HBM per device.

v0:
```python
import jax
import jax.numpy as jnp
from jax import lax
from jax.sharding import PartitionSpec as P

HEADS = 6
WIN_LAT = 6
WIN_LON = 12


EPS = 1e-05


def passed_along(value, axis, steps):
    count = lax.axis_size(axis)
    pairs = [(source, (source + steps) % count) for source in range(count)]
    return lax.ppermute(value, axis, pairs)


def from_behind(value, axis, by):
    devices = lax.axis_size(axis)
    pairs = [(i, i + by) for i in range(devices) if 0 <= i + by < devices]
    return lax.ppermute(value, axis, pairs)


def from_root(value, axis, root):
    mine = lax.axis_index(axis) == root
    return lax.psum(jnp.where(mine, value, jnp.zeros_like(value)), axis)


def normalize(values, gain):
    average = jnp.mean(values, axis=-1, keepdims=True)
    centred = values - average
    spread = jnp.mean(centred * centred, axis=-1, keepdims=True)
    return centred * lax.rsqrt(spread + EPS) * gain


def to_windows(grid):
    count, levels, rows, cells, feats = grid.shape
    shaped = grid.reshape(count, levels, rows // WIN_LAT, WIN_LAT, cells // WIN_LON, WIN_LON, feats)
    shaped = shaped.transpose(0, 2, 4, 1, 3, 5, 6)
    return shaped.reshape(
        count, rows // WIN_LAT, cells // WIN_LON, levels * WIN_LAT * WIN_LON, feats
    )


def from_windows(windows, levels):
    count, lat_count, lon_count, tokens, feats = windows.shape
    shaped = windows.reshape(count, lat_count, lon_count, levels, WIN_LAT, WIN_LON, feats)
    shaped = shaped.transpose(0, 3, 1, 4, 2, 5, 6)
    return shaped.reshape(count, levels, lat_count * WIN_LAT, lon_count * WIN_LON, feats)


def attend(source, gain_first, w_qkv, w_out, bias_table):
    count, levels, rows, cells, width = source.shape
    head_dim = width // HEADS
    normed_a = normalize(source.astype(jnp.float32), gain_first[:, None, None, None, :]).astype(
        jnp.bfloat16
    )
    packed = jnp.einsum(
        "szhlc,scd->szhld", normed_a, w_qkv, preferred_element_type=jnp.float32
    ).astype(jnp.bfloat16)
    windows = to_windows(packed)
    _, lat_count, lon_count, tokens, _ = windows.shape
    queries = windows[..., :width].reshape(count, lat_count, lon_count, tokens, HEADS, head_dim)
    keys = windows[..., width : 2 * width].reshape(
        count, lat_count, lon_count, tokens, HEADS, head_dim
    )
    values = windows[..., 2 * width :].reshape(count, lat_count, lon_count, tokens, HEADS, head_dim)
    scores = jnp.einsum("sanqhd,sankhd->sanhqk", queries, keys, preferred_element_type=jnp.float32)
    scores = scores * head_dim ** (-0.5) + bias_table[:, :, None]
    highest = jnp.max(scores, axis=-1, keepdims=True)
    expo = jnp.exp(scores - highest)
    probs = (expo / jnp.sum(expo, axis=-1, keepdims=True)).astype(jnp.bfloat16)
    context = jnp.einsum("sanhqk,sankhd->sanqhd", probs, values, preferred_element_type=jnp.float32)
    context = context.astype(jnp.bfloat16).reshape(count, lat_count, lon_count, tokens, width)
    grid = from_windows(context, levels)
    return jnp.einsum("szhlc,scd->szhld", grid, w_out, preferred_element_type=jnp.float32).astype(
        jnp.bfloat16
    )


def cut_band(extended, starts, width):
    return jax.vmap(lambda block, begin: lax.dynamic_slice_in_dim(block, begin, width, 2))(
        extended, starts
    )


def section_pair(sections, shifts, gain_pairs, w_qkv, w_out, w_up, w_down, bias_table):
    width_cells = sections.shape[3]
    beyond = passed_along(sections, "lon", -1)
    extended = jnp.concatenate([sections, beyond], axis=3)
    rolled = cut_band(extended, shifts, width_cells)
    attended = attend(rolled, gain_pairs[:, 0], w_qkv, w_out, bias_table)
    before = passed_along(attended, "lon", 1)
    joined = jnp.concatenate([before, attended], axis=3)
    restored = cut_band(joined, width_cells - shifts, width_cells)
    first_sum = sections.astype(jnp.float32) + restored.astype(jnp.float32)
    normed_b = normalize(first_sum, gain_pairs[:, 1][:, None, None, None, :]).astype(jnp.bfloat16)
    hidden = jax.nn.gelu(
        jnp.einsum("szhlc,scf->szhlf", normed_b, w_up, preferred_element_type=jnp.float32)
    )
    hidden = hidden.astype(jnp.bfloat16)
    output = first_sum + jnp.einsum(
        "szhlf,sfc->szhlc", hidden, w_down, preferred_element_type=jnp.float32
    )
    return output.astype(jnp.bfloat16)


def per_device(
    fields,
    entry_order,
    shift_offsets,
    qkv_weight,
    out_weight,
    up_weight,
    down_weight,
    attn_bias,
    norm_gain,
):
    segments = lax.axis_size("segment")
    position = lax.axis_index("segment")
    micro_count = fields.shape[0]
    band_shape = fields.shape[1:]
    gain_pairs = norm_gain[:, 0]
    w_qkv = qkv_weight[:, 0]
    w_out = out_weight[:, 0]
    w_up = up_weight[:, 0]
    w_down = down_weight[:, 0]
    bias_table = attn_bias[:, 0]
    offset_table = shift_offsets[:, :, 0]
    tick_count = micro_count + 2 * segments - 1

    def tick(moment, carried):
        enc_in, dec_in, stored, results = carried
        slot_enc = moment - position
        slot_dec = moment - (2 * segments - 1 - position)
        enc_index = jnp.clip(slot_enc, 0, micro_count - 1)
        dec_index = jnp.clip(slot_dec, 0, micro_count - 1)
        entering = lax.dynamic_index_in_dim(
            fields, entry_order[jnp.clip(moment, 0, micro_count - 1)], 0, keepdims=False
        )
        enc_source = jnp.where(position == 0, entering, enc_in)
        skipped = lax.dynamic_index_in_dim(stored, dec_index, 0, keepdims=False)
        merged = (0.5 * (dec_in.astype(jnp.float32) + skipped.astype(jnp.float32))).astype(
            jnp.bfloat16
        )
        dec_source = jnp.where(position < segments - 1, merged, dec_in)
        sections = jnp.stack([enc_source, dec_source])
        shifts = jnp.stack([offset_table[enc_index, 0], offset_table[dec_index, 1]])
        produced = section_pair(
            sections, shifts, gain_pairs, w_qkv, w_out, w_up, w_down, bias_table
        )
        enc_out = produced[0]
        dec_out = produced[1]
        valid_enc = (slot_enc >= 0) & (slot_enc < micro_count)
        current_kept = lax.dynamic_index_in_dim(stored, enc_index, 0, keepdims=False)
        stored = lax.dynamic_update_index_in_dim(
            stored, jnp.where(valid_enc, enc_out, current_kept), enc_index, 0
        )
        valid_dec = (slot_dec >= 0) & (slot_dec < micro_count) & (position == 0)
        target = entry_order[dec_index]
        current_result = lax.dynamic_index_in_dim(results, target, 0, keepdims=False)
        results = lax.dynamic_update_index_in_dim(
            results, jnp.where(valid_dec, dec_out, current_result), target, 0
        )
        lowered = from_behind(enc_out, "segment", 1)
        raised = from_behind(dec_out, "segment", -1)
        next_dec = jnp.where(position == segments - 1, enc_out, raised)
        return (lowered, next_dec, stored, results)

    empty_band = jnp.zeros(band_shape, jnp.bfloat16)
    empty_stack = jnp.zeros((micro_count,) + band_shape, jnp.bfloat16)
    _, _, _, results = lax.fori_loop(
        0, tick_count, tick, (empty_band, empty_band, empty_stack, empty_stack)
    )
    delivered = from_root(results, "segment", 0)
    share = delivered.shape[4] // segments
    return lax.dynamic_slice_in_dim(delivered, position * share, share, 4)


def solution(mesh):
    placed = (
        P(None, None, None, "lon", None),
        P(),
        P(None, None, "segment"),
        P(None, "segment", None, None),
        P(None, "segment", None, None),
        P(None, "segment", None, None),
        P(None, "segment", None, None),
        P(None, "segment", None, None, None, None),
        P(None, "segment", None, None),
    )
    return jax.shard_map(
        per_device,
        mesh=mesh,
        in_specs=placed,
        out_specs=P(None, None, None, "lon", "segment"),
        check_vma=False,
    )
```

profile of v0, /device:TPU:4, one launch (start us, length us, event | category | flops | bytes accessed | tf_op | source)
XLA Modules:
  0.0 1210.6 jit_solution(12263965731393615058)
XLA Ops:
  14.3 1093.5 %while.22 = (s32[]{:T(128)}, bf16[2,12,12,192]{3,2,1,0:T(8,128)(2,1)S(1)}, bf16[2,12,12,192]{3,2,1,0:T(8,128)(2,1)}, bf16[4,2,12,12,192]{4,3,2,1,0:T(8,128)(2,1)...) while((s32[]{:T(128)}, ...), condition=%wide.region_7.8_spmd.clone, body=%wide.region_0.7_spmd.clone.sunk | while | flops 588575552 | bytes 37115332 | solution.py:174
  52.7 7.1 collective-permute-done.1
  110.3 7.1 collective-permute-done.1
  167.5 7.1 collective-permute-done.1
  224.4 7.1 collective-permute-done.1
  281.6 7.1 collective-permute-done.1
  296.3 6.8 collective-permute-start.2
  338.8 7.1 collective-permute-done.1
  353.5 6.8 collective-permute-start.2
  396.1 7.1 collective-permute-done.1
  410.8 6.8 collective-permute-start.2
  453.3 7.1 collective-permute-done.1
  468.0 6.8 collective-permute-start.2
  510.6 7.1 collective-permute-done.1
  525.3 6.8 collective-permute-start.2
  567.8 7.1 collective-permute-done.1
  582.5 6.8 collective-permute-start.2
  625.1 7.1 collective-permute-done.1
  682.3 7.1 collective-permute-done.1
  697.0 6.8 collective-permute-start.2
  739.6 7.1 collective-permute-done.1
  754.3 6.8 collective-permute-start.2
  796.8 7.1 collective-permute-done.1
  811.5 6.8 collective-permute-start.2
  854.1 7.1 collective-permute-done.1
  911.3 7.1 collective-permute-done.1
  926.0 6.8 collective-permute-start.2
  968.6 7.1 collective-permute-done.1
  1025.8 7.1 collective-permute-done.1
  1083.1 7.1 collective-permute-done.1
  1097.8 6.8 collective-permute-start.2
  1109.0 92.5 %all-reduce.2.cloned.1.call-done = bf16[4,2,12,12,192]{4,1,3,2,0:T(2,128)(2,1)} async-done(((bf16[4,2,12,12,192]{4,1,3,2,0:T(2,128)(2,1)}), bf16[4,2,12,12,192]{4,1,3,2,0:T(2,128)(2,1)}) %all-reduce.2.cloned.1.call-update) | async-done | bytes 442384 | tf_op jit(solution)/shard_map/psum | solution.py:28
  (1183 shorter events, 813.7 us)
Async XLA Ops:
  6.5 1195.1 %all-reduce.2.cloned.1.call-start = ((), (), s32[]{:S(2)}) async-start(), calls=%async_computation | async-start | bytes 1179648 | tf_op jit(solution)/shard_map/psum | solution.py:28
  19.3 11.3 collective-permute-start
  122.3 11.1 collective-permute-start.3
  179.5 11.5 collective-permute-start.3
  236.4 11.8 collective-permute-start.3
  293.5 11.9 collective-permute-start.3
  296.3 10.0 collective-permute-start.2
  350.8 11.9 collective-permute-start.3
  353.5 10.0 collective-permute-start.2
  408.0 11.9 collective-permute-start.3
  410.8 10.0 collective-permute-start.2
  465.3 11.9 collective-permute-start.3
  468.0 10.0 collective-permute-start.2
  522.5 11.9 collective-permute-start.3
  525.3 10.0 collective-permute-start.2
  579.8 11.9 collective-permute-start.3
  582.5 10.0 collective-permute-start.2
  637.0 11.9 collective-permute-start.3
  639.8 10.0 collective-permute-start.2
  694.3 11.9 collective-permute-start.3
  697.0 10.0 collective-permute-start.2
  751.5 11.9 collective-permute-start.3
  754.3 10.0 collective-permute-start.2
  808.8 11.9 collective-permute-start.3
  811.5 10.0 collective-permute-start.2
  866.0 12.0 collective-permute-start.3
  923.3 11.9 collective-permute-start.3
  926.0 10.0 collective-permute-start.2
  980.5 11.9 collective-permute-start.3
  1037.8 11.9 collective-permute-start.3
  1095.0 11.9 collective-permute-start.3
  1097.8 10.0 collective-permute-start.2
  (181 other events, 1411.2 us)
Sparse Core Ops, SparseCore 0:
  1109.2 92.3 all-reduce.1
where the time goes:
time: 1220 us; the launch traced here: 1210 us
  waiting for transfers between devices  300 us (25%)
  local copies, waits for them, and re-layouts  288 us (24%)
  other arithmetic  187 us (15%)
  starting transfers between devices  174 us (14%)
  matrix products  167 us (14%)
  loops' own time  81.8 us (7%)
  between operations  13.4 us (1%)
    ppermute x38, starting transfers between devices, from_behind(): return lax.ppermute(value, axis, pairs)  164 us
    ppermute x38, waiting for transfers between devices, passed_along(): return lax.ppermute(value, axis, pairs)  160 us
    psum x1, waiting for transfers between devices, from_root(): return lax.psum(jnp.where(mine, value, jnp.zeros_like(value)), axis)  92.5 us
    another operation x1, loops' own time, per_device(): lax.fori_loop(0, tick_count, tick, (empty_band, empty_band, empty_stack,...  81.8 us
    dot_general x19, matrix products, attend(): jnp.einsum('sanqhd,sankhd->sanhqk', queries, keys, preferred_element_type...  55.5 us
    dot_general x19, matrix products, attend(): jnp.einsum('sanhqk,sankhd->sanqhd', probs, values, preferred_element_type...  51.3 us
    gather x38, other arithmetic, cut_band(): lax.dynamic_slice_in_dim(block, begin, width, 2)  51.1 us
    slice x38, local copies, waits for them, and re-layouts, attend(): windows[..., width:2 * width]  48.4 us
  transfers between devices with their start and end apart: 77, of which 61 were waited for; matrix products, arithmetic and copies ran while one was open for 9% of the time, Pallas kernels for 0%

commit v1 on v0

v1 whole, which is shorter than its diff:
```python
import functools
import math

import jax
import jax.numpy as jnp
from jax import lax
from jax.experimental import pallas as pl
from jax.experimental.pallas import tpu as pltpu
from jax.sharding import PartitionSpec as P

BF = jnp.bfloat16
F32 = jnp.float32
MESH = pl.DeviceIdType.MESH
NT = (((1,), (1,)), ((), ()))
TN = (((0,), (0,)), ((), ()))
NN = (((1,), (0,)), ((), ()))

SEGS = 8
SECTIONS = 16
HEADS = 6
TOK = 144
WIDTH = 192
LON = 12
STRIP = 192
HALF_W = 9 * STRIP
HALF_B = 4 * TOK
HALF = HALF_W + HALF_B
PACK = 2 * HALF
PARAMS = HALF + HALF_W + 3 * TOK
EPS = 1e-5
QSCALE = math.log2(math.e) / math.sqrt(32.0)


def dot(a, b, dims=NN):
    return lax.dot_general(a, b, dims, preferred_element_type=F32)


def side(parts):
    return jnp.concatenate(parts, axis=1)


def down(parts):
    return jnp.concatenate(parts, axis=0)


def lanes(shape):
    return lax.broadcasted_iota(jnp.int32, shape, len(shape) - 1)


def normalize(x, gain, inside):
    mean = jnp.sum(x, axis=-1, keepdims=True) * (1.0 / WIDTH)
    centred = x - mean * inside
    spread = jnp.sum(centred * centred, axis=-1, keepdims=True) * (1.0 / WIDTH)
    return (centred * lax.rsqrt(spread + EPS) * gain).astype(BF)


def pick(lon, shift):
    row = lax.broadcasted_iota(jnp.int32, (TOK, 128), 0).astype(F32)
    x = lon + shift
    wrap = jnp.where(x < 0, float(LON - TOK), jnp.where(x > LON - 1, float(TOK - LON), 0.0))
    target = row + shift + wrap + float(TOK)
    col = lanes((TOK, 128)).astype(F32)
    tiles = [jnp.where(col + float(128 * j) == target, 1.0, 0.0).astype(BF) for j in range(4)]
    return side(tiles)[:, : 3 * TOK]


def section(u, strip, bias, gain_a, gain_b):
    col = lanes((1, 256))
    inside = jnp.where(col < WIDTH, 1.0, 0.0)
    low = jnp.where(lanes((1, 128)) < 64, 1.0, 0.0)
    normed = normalize(u, gain_a, inside)
    short = normed[:, :WIDTH]
    qk = dot(short, side([strip(0), strip(1), strip(2)]))
    qb = (qk[:, :256] * QSCALE).astype(BF)
    kb = side([qk[:, 256:], pltpu.roll(qk[:, 128:256], 64, 1)]).astype(BF)
    mixed = strip(4)
    vt = dot(side([strip(3), mixed]), normed, NT).astype(BF)
    zero = jnp.zeros((TOK, 256), BF)
    pos = lanes((TOK, 256))
    spread_q = down(
        [jnp.where((pos >= 32 * h) & (pos < 32 * h + 32), qb, zero) for h in range(HEADS)]
        + [jnp.zeros((32, 256), BF)]
    )
    scores = dot(kb, spread_q, NT) + side([bias(j) for j in range(7)]).astype(F32)
    top = jnp.max(scores, axis=0, keepdims=True)
    expo = jnp.exp2(scores - top)
    inverse = 1.0 / jnp.sum(expo, axis=0, keepdims=True)
    expo = expo.astype(BF)
    parts = []
    for h in range(HEADS):
        cut = slice(128 * h, 128 * h + 256)
        part = dot(vt[32 * h : 32 * h + 32], expo[:, cut]) * inverse[:, cut]
        if h:
            part = pltpu.roll(part, 256 - 16 * h, 1)
        parts.append(part[:, :TOK])
    context = down(parts).astype(BF)
    out = dot(context, side([strip(5), mixed]), TN)
    out = side([out[:, :128], pltpu.roll(out[:, 128:], 64, 1) * low])
    x1 = u + out.astype(BF).astype(F32)
    normed = normalize(x1, gain_b, inside)[:, :WIDTH]
    hidden = jax.nn.gelu(dot(normed, side([strip(6 + j) for j in range(6)]))).astype(BF)
    tail = down([strip(16), strip(17)])
    y0 = dot(hidden[:, :384], side([down([strip(12), strip(13)]), tail]))
    y1 = dot(hidden[:, 384:], side([down([strip(14), strip(15)]), tail]))
    y = side([y0[:, :128] + y1[:, :128], (y0[:, 128:] + pltpu.roll(y1[:, 128:], 64, 1)) * low])
    return (x1 + y).astype(BF)


def kernel(
    x_ref, own_ref, other_ref, out_ref,
    packs, hist, lon_ref, pieces, received,
    local_sem, w_send, w_recv, s_send, s_recv, h_send, h_recv, f_send, f_recv,
):
    seg = lax.axis_index("segment")
    me = lax.axis_index("lon")
    ring = lax.axis_size("lon")
    core = lax.rem(me, 2)
    sibling = me + 1 - 2 * core
    west = lax.rem(me + ring - 1, ring)
    east = lax.rem(me + 1, ring)
    slot = seg // 2
    lat = lax.rem(seg, 2)

    fills = [
        pltpu.make_async_copy(
            own_ref.at[half], packs.at[seg if half == 0 else 15 - seg], local_sem.at[half]
        )
        for half in range(2)
    ]
    for fill in fills:
        fill.start()

    barrier = pltpu.get_barrier_semaphore()
    for d in range(1, SEGS):
        pl.semaphore_signal(
            barrier, inc=1, device_id=(lax.rem(seg + d, SEGS), me), device_id_type=MESH
        )
    for lon_to in (west, east):
        pl.semaphore_signal(barrier, inc=1, device_id=(seg, lon_to), device_id_type=MESH)
    pl.semaphore_wait(barrier, SEGS + 1)

    def source(number):
        return jnp.minimum(number, SECTIONS - 1 - number)

    def weight_copy(half, d, number):
        there = lax.rem(seg + d, SEGS)
        start = pl.multiple_of(core * HALF, 16)
        return pltpu.make_async_remote_copy(
            packs.at[number, pl.ds(start, HALF)],
            packs.at[number, pl.ds(start, HALF)],
            w_send.at[half, d],
            w_recv.at[number],
            device_id=(there, me),
            device_id_type=MESH,
        )

    def send_weights(half):
        number = seg if half == 0 else 15 - seg
        start = pl.multiple_of(core * HALF, 16)
        b_start = pl.multiple_of(core * HALF + HALF_W, 16)
        for d in (1, 7, 2, 6, 3, 5, 4):
            there = lax.rem(seg + d, SEGS)
            if d % 2 == 0:
                weight_copy(half, d, number).start()
            else:
                pltpu.make_async_remote_copy(
                    packs.at[number, pl.ds(start, HALF_W)],
                    packs.at[number, pl.ds(start, HALF_W)],
                    w_send.at[half, d],
                    w_recv.at[number],
                    device_id=(there, me),
                    device_id_type=MESH,
                ).start()
                pltpu.make_async_remote_copy(
                    other_ref.at[half, core],
                    packs.at[number, pl.ds(b_start, HALF_B)],
                    w_send.at[half, d],
                    w_recv.at[number],
                    device_id=(there, me),
                    device_id_type=MESH,
                ).start()

    def relay_copy(number):
        start = pl.multiple_of(core * HALF, 16)
        return pltpu.make_async_remote_copy(
            packs.at[number, pl.ds(start, HALF)],
            packs.at[number, pl.ds(start, HALF)],
            s_send.at[number],
            s_recv.at[number],
            device_id=(seg, sibling),
            device_id_type=MESH,
        )

    def relay_wait(number):
        start = pl.multiple_of((1 - core) * HALF, 16)
        pltpu.make_async_remote_copy(
            packs.at[number, pl.ds(start, HALF)],
            packs.at[number, pl.ds(start, HALF)],
            s_send.at[number],
            s_recv.at[number],
            device_id=(seg, sibling),
            device_id_type=MESH,
        ).wait_recv()

    def relay(number):
        @pl.when(source(number) != seg)
        def _():
            weight_copy(0, 1, number).wait_recv()
            relay_copy(number).start()

    def halo_copy(number, way):
        return pltpu.make_async_remote_copy(
            hist.at[number, pl.ds(TOK, TOK)],
            hist.at[number, pl.ds(2 * TOK if way == 0 else 0, TOK)],
            h_send.at[number, way],
            h_recv.at[number, way],
            device_id=(seg, west if way == 0 else east),
            device_id_type=MESH,
        )

    hist[0, TOK : 2 * TOK] = x_ref[...]
    for way in range(2):
        halo_copy(0, way).start()
    for fill in fills:
        fill.wait()
    send_weights(0)
    token = lax.broadcasted_iota(jnp.int32, (TOK, 128), 0)
    lon_ref[...] = lax.rem(token, LON).astype(F32)
    relay(0)

    def params(number):
        return packs[number, PARAMS : PARAMS + 16, :].astype(F32)

    def offset(tile):
        row = lax.broadcasted_iota(jnp.int32, (16, 128), 0)
        return jnp.sum(jnp.where(row == 12 + slot, tile, 0.0), axis=0, keepdims=True)

    def step(number, decoder):
        if not decoder:
            @pl.when(number == 0)
            def _():
                send_weights(1)

        @pl.when(number < SECTIONS - 1)
        def _():
            relay(number + 1)

        @pl.when(source(number) != seg)
        def _():
            relay_wait(number)

        tile = params(number)
        now = offset(tile)
        if decoder:
            before = offset(params(number - 1))
            aside = dot(pick(lon_ref[...], now - offset(params(15 - number))), hist[16 - number])
        else:
            before = offset(params(jnp.maximum(number - 1, 0)))
            before = before * jnp.where(number > 0, 1.0, 0.0)
        chosen = pick(lon_ref[...], now - before)
        for way in range(2):
            halo_copy(number, way).wait_recv()
        u = dot(chosen, hist[number])
        if decoder:
            u = ((u + aside) * 0.5).astype(BF).astype(F32)
        gain_a = side([tile[0:1] + tile[2:3] + tile[4:5], tile[1:2] + tile[3:4] + tile[5:6]])
        gain_b = side([tile[6:7] + tile[8:9] + tile[10:11], tile[7:8] + tile[9:10] + tile[11:12]])

        def strip(j):
            start = STRIP * j if j < 9 else HALF + STRIP * (j - 9)
            return packs[number, start : start + STRIP, :]

        def bias(j):
            start = HALF_W + TOK * j if j < 4 else HALF + HALF_W + TOK * (j - 4)
            return packs[number, start : start + TOK, :]

        hist[number + 1, TOK : 2 * TOK] = section(u, strip, bias, gain_a, gain_b)
        for way in range(2):
            halo_copy(number + 1, way).start()

    lax.fori_loop(0, 9, lambda i, c: (step(i, False), c)[1], 0)
    lax.fori_loop(9, SECTIONS, lambda i, c: (step(i, True), c)[1], 0)

    back = pick(lon_ref[...], -offset(params(SECTIONS - 1)))
    for way in range(2):
        halo_copy(SECTIONS, way).wait_recv()
    final = dot(back, hist[SECTIONS])
    share = WIDTH // SEGS
    for s in range(SEGS):
        pieces[s, :, :share] = final[:, share * s : share * (s + 1)].astype(BF)

    def piece_copy(d):
        there = lax.rem(seg + d, SEGS)
        return pltpu.make_async_remote_copy(
            pieces.at[there],
            received.at[seg],
            f_send.at[d],
            f_recv.at[d],
            device_id=(there, me),
            device_id_type=MESH,
        )

    for d in range(1, SEGS):
        piece_copy(d).start()
    mine = pltpu.make_async_copy(pieces.at[seg], received.at[seg], local_sem.at[0])
    mine.start()

    for half in range(2):
        number = seg if half == 0 else 15 - seg
        for d in range(1, SEGS):
            weight_copy(half, d, number).wait_send()
    for number in range(SECTIONS):
        @pl.when(source(number) != seg)
        def _():
            relay_copy(number).wait_send()
    for number in range(SECTIONS + 1):
        for way in range(2):
            halo_copy(number, way).wait_send()
    mine.wait()
    for d in range(1, SEGS):
        piece_copy(d).wait()
    out_ref[...] = received[...]


def split3(x):
    high = x.astype(BF)
    rest = x - high.astype(F32)
    middle = rest.astype(BF)
    return high, middle, (rest - middle.astype(F32)).astype(BF)


def pack_weights(qkv, out, up, low, gains, shifts, bias, lat):
    q, k, v = qkv[:, :192], qkv[:, 192:384], qkv[:, 384:].T
    strips = [
        q[:, :128], side([q[:, 128:], k[:, 128:]]), k[:, :128],
        v[:, :128], side([v[:, 128:], out[:, 128:]]), out[:, :128],
    ]
    strips += [up[:, 128 * j : 128 * j + 128] for j in range(6)]
    strips += [low[:, :128], side([low[:384, 128:], low[384:, 128:]])]
    weights = down(strips).reshape(2, HALF_W, 128)
    top = jnp.max(bias, axis=-1, keepdims=True)
    bias = ((bias - top) * math.log2(math.e)).astype(BF)
    bias = bias.transpose(0, 3, 1, 2).reshape(2, TOK, HEADS * TOK)
    bias = jnp.pad(bias, ((0, 0), (0, 0), (0, 1024 - HEADS * TOK)))
    bias = bias.reshape(2, TOK, 8, 128).transpose(0, 2, 1, 3)
    rows = []
    for gain in gains:
        for part in split3(gain):
            rows += [part[:128], jnp.pad(part[128:], (0, 64))]
    rows += [jnp.full((128,), shifts[t]).astype(BF) for t in range(4)]
    small = jnp.stack(rows)
    bias = bias.reshape(2, 8 * TOK, 128)
    bias = jnp.concatenate(
        [bias[:, : 7 * TOK], jnp.broadcast_to(small, (2, 16, 128)), bias[:, 7 * TOK + 16 :]], axis=1
    ).reshape(2, 2, HALF_B, 128)
    here = lax.dynamic_index_in_dim(bias, lat, 0, keepdims=False)
    there = lax.dynamic_index_in_dim(bias, 1 - lat, 0, keepdims=False)
    own = jnp.concatenate([weights, here], axis=1).reshape(PACK, 128)
    return own, there


def per_device(
    fields, entry_order, shift_offsets, qkv_weight, out_weight, up_weight, down_weight,
    attn_bias, norm_gain,
):
    seg = lax.axis_index("segment")
    slot, lat = seg // 2, lax.rem(seg, 2)
    grid = lax.dynamic_slice(
        fields, (entry_order[slot], 0, 6 * lat, 0, 0), (1, 2, 6, LON, WIDTH)
    )
    x = jnp.pad(grid.reshape(TOK, WIDTH), ((0, 0), (0, 64)))
    packed = [
        pack_weights(
            qkv_weight[h, 0], out_weight[h, 0], up_weight[h, 0], down_weight[h, 0],
            norm_gain[h, 0], shift_offsets[:, h, 0], attn_bias[h, 0], lat,
        )
        for h in range(2)
    ]
    own = jnp.stack([p[0] for p in packed])
    other = jnp.stack([p[1] for p in packed])
    dma = pltpu.SemaphoreType.DMA
    got = pl.pallas_call(
        kernel,
        out_shape=jax.ShapeDtypeStruct((SEGS, TOK, 128), BF),
        in_specs=[pl.BlockSpec(memory_space=pltpu.VMEM), pl.BlockSpec(memory_space=pl.ANY),
                  pl.BlockSpec(memory_space=pl.ANY)],
        out_specs=pl.BlockSpec(memory_space=pltpu.VMEM),
        scratch_shapes=[
            pltpu.VMEM((SECTIONS, PACK, 128), BF),
            pltpu.VMEM((SECTIONS + 1, 3 * TOK, 256), BF),
            pltpu.VMEM((TOK, 128), F32),
            pltpu.VMEM((SEGS, TOK, 128), BF),
            pltpu.VMEM((SEGS, TOK, 128), BF),
            dma((2,)), dma((2, SEGS)), dma((SECTIONS,)), dma((SECTIONS,)), dma((SECTIONS,)),
            dma((SECTIONS + 1, 2)), dma((SECTIONS + 1, 2)), dma((SEGS,)), dma((SEGS,)),
        ],
        compiler_params=pltpu.CompilerParams(
            collective_id=0, has_side_effects=True, vmem_limit_bytes=50 * 2**20
        ),
        name="sections",
    )(x, own, other)
    share = WIDTH // SEGS
    got = got[:, :, :share].reshape(4, 2, 2, 6, LON, share).transpose(0, 2, 1, 3, 4, 5)
    got = got.reshape(4, 2, 12, LON, share)
    chosen = (entry_order[None, :] == jnp.arange(4)[:, None]).astype(jnp.int32)
    place = jnp.sum(chosen * jnp.arange(4)[None, :], axis=1)
    return jnp.take(got, place, axis=0)


def solution(mesh):
    placed = (
        P(None, None, None, "lon", None),
        P(),
        P(None, None, "segment"),
        P(None, "segment", None, None),
        P(None, "segment", None, None),
        P(None, "segment", None, None),
        P(None, "segment", None, None),
        P(None, "segment", None, None, None, None),
        P(None, "segment", None, None),
    )
    return jax.shard_map(
        per_device,
        mesh=mesh,
        in_specs=placed,
        out_specs=P(None, None, None, "lon", "segment"),
        check_vma=False,
    )
```

time: 1220 us -> 230 us (0.19)
  waiting for transfers between devices: 300 us -> 0 us
  local copies, waits for them, and re-layouts: 288 us -> 35 us
  Pallas kernels: 0 us -> 179 us
  other arithmetic: 187 us -> 12.3 us
  starting transfers between devices: 174 us -> 0 us
  matrix products: 167 us -> 0 us
  loops' own time: 81.8 us -> 0 us
    ppermute x76 -> x0, waiting for transfers between devices: 207 us -> none  [the longest x38 160 us: passed_along(): return lax.ppermute(value, axis, pairs)]
    pallas_call x0 -> x1, Pallas kernels: none -> 179 us  [per_device(): pl.pallas_call(kernel, out_shape=jax.ShapeDtypeStruct((SEGS, TOK, 128), B...]
    ppermute x76 -> x0, starting transfers between devices: 174 us -> none  [the longest x38 164 us: from_behind(): return lax.ppermute(value, axis, pairs)]
    dot_general x95 -> x0, matrix products: 167 us -> none  [the longest x19 55.5 us: attend(): jnp.einsum('sanqhd,sankhd->sanhqk', queries, keys, preferred_element_type...]
    slice x76 -> x34, local copies, waits for them, and re-layouts: 104 us -> 3.62 us  [the longest x1 1.1 us: per_device(): qkv_weight[h, 0]]
    psum x1 -> x0, waiting for transfers between devices: 92.5 us -> none  [from_root(): return lax.psum(jnp.where(mine, value, jnp.zeros_like(value)), axis)]
    another operation x1 -> x0, loops' own time: 81.8 us -> none  [per_device(): lax.fori_loop(0, tick_count, tick, (empty_band, empty_band, empty_stack,...]
    dynamic_slice x77 -> x5, local copies, waits for them, and re-layouts: 66 us -> 2.82 us  [the longest x2 1.52 us: pack_weights(): there = lax.dynamic_index_in_dim(bias, 1 - lat, 0, keepdims=False)]
  transfers between devices with their start and end apart: 77 -> 0, of which waited for: 61 -> 0; matrix products, arithmetic and copies ran while one was open for 9% -> 0% of each run, Pallas kernels for 0% -> 0%
where the time goes in v1:
time: 230 us; the launch traced here: 229 us
  Pallas kernels  179 us (78%)
  local copies, waits for them, and re-layouts  35 us (15%)
  other arithmetic  12.3 us (5%)
  between operations  2.61 us (1%)
    pallas_call x1, Pallas kernels, per_device(): pl.pallas_call(kernel, out_shape=jax.ShapeDtypeStruct((SEGS, TOK, 128), B...  179 us
    unnamed x41, local copies, waits for them, and re-layouts  15.9 us
    another operation x22, local copies, waits for them, and re-layouts, pack_weights(): small = jnp.stack(rows)  5.12 us

profile of v1, /device:TPU:4, one launch (start us, length us, event | category | flops | bytes accessed | tf_op | source)
XLA Modules:
  0.0 229.3 jit_solution(6279547463032958497)
XLA Ops:
  0.0 0.8 fusion.17
  1.0 0.7 convert.10
  1.7 0.7 fusion.18
  2.4 0.6 stack.122
  3.6 0.7 stack.124
  4.3 0.7 stack.125
  5.0 3.0 %slice_reduce_fusion.1 = (f32[2,6,144]{2,1,0:T(8,128)S(1)}, f32[2,6,144]{2,1,0:T(8,128)S(1)}) fusion(f32[2,1,2,6,144,144]{5,4,3,2,1,0:T(8,128)} %param.16), kind=kLoop, calls=%fused_computation.9 | loop fusion | flops 494208 | bytes 2004480 | tf_op jit(solution)/shard_map/reduce_max | solution.py:341
  8.1 0.6 fusion.3
  9.6 0.8 constant_dynamic-slice_fusion.1
  10.4 1.1 fusion.10
  12.0 0.6 constant_dynamic-update-slice_fusion.23
  13.3 0.6 constant_dynamic-update-slice_fusion.21
  14.6 1.0 slice_bitcast_fusion.5
  15.6 0.7 constant_dynamic-update-slice_fusion.19
  18.1 0.6 constant_dynamic-update-slice_fusion.9
  19.3 0.7 constant_dynamic-update-slice_fusion.7
  20.0 0.6 constant_dynamic-update-slice_fusion.6
  24.5 1.1 fusion.9
  25.7 0.7 slice_dynamic-update-slice_fusion.1
  26.4 0.7 maximum_dynamic-update-slice_fusion
  27.2 2.3 pad_maximum_fusion.1
  33.0 0.8 constant_dynamic-slice_fusion
  37.6 0.7 slice_dynamic-update-slice_fusion
  38.3 0.7 maximum_dynamic-update-slice_fusion.1
  39.1 1.2 pad_maximum_fusion.2
  40.6 0.7 copy-done.3
  44.1 0.7 copy.40
  44.7 1.6 reshape.92
  46.3 0.9 pad.48.x_ref
  47.2 179.4 %sections.1 = bf16[8,144,128]{2,1,0:T(8,128)(2,1)S(1)} custom-call(bf16[144,256]{1,0:T(8,128)(2,1)S(1)} %pad.48.x_ref, bf16[2,4608,128]{2,1,0:T(8,128)(2,1)S(1)} %pad_maximum_fusion.own_ref, bf16[2,2,576,128]{3,2,1,0:T(8,128)(2,1)S(1)} %pad_maximum_fusion.5.other_ref), custom_call_target="tpu_custom_call" | custom-call | tf_op jit(solution)/shard_map/sections/pallas_call | solution.py:382
  227.1 1.1 gather_fusion
  228.3 1.0 broadcast_select_fusion
  (116 shorter events, 18.6 us)
Async XLA Ops:
  0.0 44.0 %copy-start = (bf16[4,2,12,12,192]{4,1,3,2,0:T(2,128)(2,1)S(1)}, bf16[4,2,12,12,192]{4,1,3,2,0:T(2,128)(2,1)}, u32[]{:S(2)}) copy-start(bf16[4,2,12,12,192]{4,1,3,2,0:T(2,128)(2,1)} %param.9) | copy-start | bytes 1327108
  5.0 3.1 %copy-start.1 = (f32[2,1,2,6,144,144]{5,4,3,2,1,0:T(8,128)S(1)}, f32[2,1,2,6,144,144]{5,4,3,2,1,0:T(8,128)}, u32[]{:S(2)}) copy-start(f32[2,1,2,6,144,144]{5,4,3,2,1,0:T(8,128)} %param.16) | copy-start | bytes 5971972
  13.9 6.7 %copy-start.5 = (bf16[2,1,192,768]{3,2,1,0:T(8,128)(2,1)S(1)}, bf16[2,1,192,768]{3,2,1,0:T(8,128)(2,1)}, u32[]{:S(2)}) copy-start(bf16[2,1,192,768]{3,2,1,0:T(8,128)(2,1)} %param.14) | copy-start | bytes 1769476
  37.6 2.7 %copy-start.2 = (bf16[2,2304,128]{2,1,0:T(8,128)(2,1)S(1)}, bf16[2,2304,128]{2,1,0:T(8,128)(2,1)}, u32[]{:S(2)}) copy-start(bf16[2,2304,128]{2,1,0:T(8,128)(2,1)} %pad_maximum_fusion.1) | copy-start | bytes 3538948
  40.3 1.0 copy-start.3
  40.3 1.0 copy-start.4
  40.3 1.1 copy-start.6

commit v2 on v1

v2 whole, which is shorter than its diff:
```python
import functools
import math

import jax
import jax.numpy as jnp
from jax import lax
from jax.experimental import pallas as pl
from jax.experimental.pallas import tpu as pltpu
from jax.sharding import PartitionSpec as P

BF = jnp.bfloat16
F32 = jnp.float32
MESH = pl.DeviceIdType.MESH
NT = (((1,), (1,)), ((), ()))
TN = (((0,), (0,)), ((), ()))
NN = (((1,), (0,)), ((), ()))

SEGS = 8
SECTIONS = 16
EARLY = 3
HEADS = 6
TOK = 144
WIDTH = 192
LON = 12
STRIP = 192
HALF_W = 9 * STRIP
HALF_B = 4 * TOK
HALF = HALF_W + HALF_B
PACK = 2 * HALF
PARAMS = HALF + HALF_W + 3 * TOK
EPS = 1e-5
QSCALE = math.log2(math.e) / math.sqrt(32.0)


def dot(a, b, dims=NN):
    return lax.dot_general(a, b, dims, preferred_element_type=F32)


def side(parts):
    return jnp.concatenate(parts, axis=1)


def down(parts):
    return jnp.concatenate(parts, axis=0)


def lanes(shape):
    return lax.broadcasted_iota(jnp.int32, shape, len(shape) - 1)


def normalize(x, gain, inside):
    mean = jnp.sum(x, axis=-1, keepdims=True) * (1.0 / WIDTH)
    centred = x - mean * inside
    spread = jnp.sum(centred * centred, axis=-1, keepdims=True) * (1.0 / WIDTH)
    return (centred * lax.rsqrt(spread + EPS) * gain).astype(BF)


def pick(lon, shift):
    row = lax.broadcasted_iota(jnp.int32, (TOK, 128), 0).astype(F32)
    x = lon + shift
    wrap = jnp.where(x < 0, float(LON - TOK), jnp.where(x > LON - 1, float(TOK - LON), 0.0))
    target = row + shift + wrap + float(TOK)
    col = lanes((TOK, 128)).astype(F32)
    tiles = [jnp.where(col + float(128 * j) == target, 1.0, 0.0).astype(BF) for j in range(4)]
    return side(tiles)[:, : 3 * TOK]


def section(u, strip, bias, gain_a, gain_b):
    col = lanes((1, 256))
    inside = jnp.where(col < WIDTH, 1.0, 0.0)
    low = jnp.where(lanes((1, 128)) < 64, 1.0, 0.0)
    normed = normalize(u, gain_a, inside)
    short = normed[:, :WIDTH]
    qk = dot(short, side([strip(0), strip(1), strip(2)]))
    qb = (qk[:, :256] * QSCALE).astype(BF)
    kb = side([qk[:, 256:], pltpu.roll(qk[:, 128:256], 64, 1)]).astype(BF)
    mixed = strip(4)
    vt = dot(side([strip(3), mixed]), normed, NT).astype(BF)
    zero = jnp.zeros((TOK, 256), BF)
    pos = lanes((TOK, 256))
    spread_q = down(
        [jnp.where((pos >= 32 * h) & (pos < 32 * h + 32), qb, zero) for h in range(HEADS)]
        + [jnp.zeros((32, 256), BF)]
    )
    scores = dot(kb, spread_q, NT) + side([bias(j) for j in range(7)]).astype(F32)
    top = jnp.max(scores, axis=0, keepdims=True)
    expo = jnp.exp2(scores - top)
    inverse = 1.0 / jnp.sum(expo, axis=0, keepdims=True)
    expo = expo.astype(BF)
    parts = []
    for h in range(HEADS):
        cut = slice(128 * h, 128 * h + 256)
        part = dot(vt[32 * h : 32 * h + 32], expo[:, cut]) * inverse[:, cut]
        if h:
            part = pltpu.roll(part, 256 - 16 * h, 1)
        parts.append(part[:, :TOK])
    context = down(parts).astype(BF)
    out = dot(context, side([strip(5), mixed]), TN)
    out = side([out[:, :128], pltpu.roll(out[:, 128:], 64, 1) * low])
    x1 = u + out.astype(BF).astype(F32)
    normed = normalize(x1, gain_b, inside)[:, :WIDTH]
    hidden = jax.nn.gelu(dot(normed, side([strip(6 + j) for j in range(6)]))).astype(BF)
    tail = down([strip(16), strip(17)])
    y0 = dot(hidden[:, :384], side([down([strip(12), strip(13)]), tail]))
    y1 = dot(hidden[:, 384:], side([down([strip(14), strip(15)]), tail]))
    y = side([y0[:, :128] + y1[:, :128], (y0[:, 128:] + pltpu.roll(y1[:, 128:], 64, 1)) * low])
    return (x1 + y).astype(BF)


def kernel(
    fields_ref, order_ref, shift_ref, qkv_ref, out_w_ref, up_ref, low_ref, bias_ref, gain_ref,
    out_ref,
    packs, other, hist, lon_ref, stage, swap, gains, pieces, received,
    local_sem, swap_sem, a_send, a_recv, b_send, b_recv, x_send, x_recv,
    c_send, c_recv, w_send, w_recv, s_send, s_recv, h_send, h_recv, f_send, f_recv,
):
    seg = lax.axis_index("segment")
    me = lax.axis_index("lon")
    ring = lax.axis_size("lon")
    half_ring = ring // 2
    core = lax.rem(me, 2)
    sibling = me + 1 - 2 * core
    column = lax.rem(seg, 2)
    facing = seg + 1 - 2 * column
    slot = column + 2 * (seg // 4)
    lat = lax.rem(seg // 2, 2)
    across = lax.rem(me + half_ring, ring)
    folded = me >= half_ring

    def along(place):
        place = lax.rem(place + ring, ring)
        return jnp.where(place < half_ring, place, 3 * half_ring - 1 - place)

    place = along(me)
    west, east = along(place - 1), along(place + 1)

    barrier = pltpu.get_barrier_semaphore()

    def greet(seg_to, lon_to):
        pl.semaphore_signal(barrier, inc=1, device_id=(seg_to, lon_to), device_id_type=MESH)

    for d in (2, 4, 6):
        greet(lax.rem(seg + d, SEGS), me)
    greet(facing, across)
    greet(seg, west)
    greet(seg, east)
    for d in range(1, SEGS):
        greet(lax.rem(seg + d, SEGS), place)
    greet(seg, jnp.where(folded, place, sibling))
    chips = half_ring // 2
    chip = lax.rem(me, half_ring) // 2
    plane = me // half_ring

    def on_chip(n):
        return plane * half_ring + 2 * lax.rem(chip + n, chips) + core

    for n in range(1, chips):
        greet(seg, on_chip(n))
    greet(seg, across)
    for n in range(1, 4):
        greet(lax.rem(facing + 2 * n, SEGS), across)

    def source(number):
        return jnp.minimum(number, SECTIONS - 1 - number)

    def own_number(half):
        return seg if half == 0 else SECTIONS - 1 - seg

    def prepare(half):
        number = own_number(half)

        def put(start, block):
            block = block.astype(BF)
            packs[number, start : start + block.shape[0], :] = block
            other[half, start : start + block.shape[0], :] = block

        def put_strip(j, block):
            put(STRIP * j if j < 9 else HALF + STRIP * (j - 9), block)

        low = lanes((STRIP, 128)) < 64
        qkv = [qkv_ref[half, :, 128 * j : 128 * j + 128].astype(F32) for j in range(4)]
        put_strip(0, qkv[0])
        put_strip(1, jnp.where(low, qkv[1], qkv[2]))
        put_strip(2, jnp.where(low, pltpu.roll(qkv[1], 64, 1), pltpu.roll(qkv[2], 64, 1)))
        eye = (lax.broadcasted_iota(jnp.int32, (WIDTH, WIDTH), 0) == lanes((WIDTH, WIDTH)))
        turned = dot(jnp.where(eye, 1.0, 0.0).astype(BF), qkv_ref[half, :, 384:576], NT)
        out_w = out_w_ref[half].astype(F32)
        put_strip(3, turned[:, :128])
        put_strip(4, side([turned[:, 128:], out_w[:, 128:]]))
        put_strip(5, out_w[:, :128])
        for j in range(6):
            put_strip(6 + j, up_ref[half, :, 128 * j : 128 * j + 128])
        for j in range(4):
            put_strip(12 + j, low_ref[half, STRIP * j : STRIP * j + STRIP, :128])
        for j in range(2):
            upper = low_ref[half, STRIP * j : STRIP * j + STRIP, 128:].astype(F32)
            lower = low_ref[half, 384 + STRIP * j : 384 + STRIP * j + STRIP, 128:].astype(F32)
            put_strip(16 + j, side([upper, lower]))

        eye = (lax.broadcasted_iota(jnp.int32, (TOK, TOK), 0) == lanes((TOK, TOK)))
        eye = jnp.where(eye, 1.0, 0.0).astype(BF)

        def put_bias(window, store):
            table = bias_ref[half, window].reshape(HEADS * TOK, TOK)
            top = jnp.max(table, axis=-1, keepdims=True)
            table = ((table - top) * math.log2(math.e)).astype(BF)
            table = dot(eye, down([table, jnp.zeros((32, TOK), BF)]), NT).astype(BF)
            for j in range(7):
                start = HALF_W + TOK * j if j < 4 else HALF + HALF_W + TOK * (j - 4)
                store(start, table[:, 128 * j : 128 * j + 128])

        def store_own(start, block):
            packs[number, start : start + TOK, :] = block

        def store_other(start, block):
            other[half, start : start + TOK, :] = block

        put_bias(lat, store_own)
        put_bias(1 - lat, store_other)
        gains[...] = jnp.zeros_like(gains)
        gains[0:2, :WIDTH] = gain_ref[half]
        rows = []
        for n in range(2):
            for part in split3(gains[n : n + 1, :]):
                rows += [part[:, :128], part[:, 128:]]
        rows += [jnp.full((1, 128), shift_ref[t, half].astype(F32)) for t in range(4)]
        put(PARAMS, down(rows))
        rest = jnp.zeros((TOK - 16, 128), BF)
        put(PARAMS + 16, rest)

    half_rows = pl.ds(pl.multiple_of(core * HALF, 16), HALF)

    def part_rows(plane_of):
        start = core * HALF + plane_of * (HALF // 2)
        return pl.ds(pl.multiple_of(start, 16), HALF // 2)

    def own_copy(half, n):
        number = own_number(half)
        ref = packs.at[number] if n == 2 else other.at[half]
        return pltpu.make_async_remote_copy(
            ref.at[half_rows], packs.at[number, half_rows], w_send.at[half, n], w_recv.at[number],
            device_id=(lax.rem(seg + 2 * n, SEGS), me), device_id_type=MESH,
        )

    def send_weights(half):
        facing_copy(own_number(half)).start()
        for n in (1, 3, 2):
            own_copy(half, n).start()

    def facing_copy(number):
        rows = part_rows(plane)
        return pltpu.make_async_remote_copy(
            packs.at[number, rows], packs.at[number, rows], c_send.at[number], c_recv.at[number],
            device_id=(facing, across), device_id_type=MESH,
        )

    def cross_copy(number, plane_of):
        rows = part_rows(plane_of)
        return pltpu.make_async_remote_copy(
            packs.at[number, rows], packs.at[number, rows], x_send.at[number], x_recv.at[number],
            device_id=(seg, across), device_id_type=MESH,
        )

    def sibling_copy(number, start):
        start = pl.multiple_of(start * HALF, 16)
        return pltpu.make_async_remote_copy(
            packs.at[number, pl.ds(start, HALF)],
            packs.at[number, pl.ds(start, HALF)],
            s_send.at[number],
            s_recv.at[number],
            device_id=(seg, sibling),
            device_id_type=MESH,
        )

    def first(number):
        seg_of = source(number)

        @pl.when((seg_of != seg) & (lax.rem(seg_of, 2) == column))
        def _():
            pltpu.make_async_remote_copy(
                packs.at[number, half_rows], packs.at[number, half_rows], w_send.at[0, 0],
                w_recv.at[number], device_id=(facing, across), device_id_type=MESH,
            ).wait_recv()
            facing_copy(number).start()
            sibling_copy(number, core).start()

    def second(number):
        @pl.when(lax.rem(source(number), 2) != column)
        def _():
            rows = part_rows(1 - plane)
            pltpu.make_async_remote_copy(
                packs.at[number, rows], packs.at[number, rows], c_send.at[number],
                c_recv.at[number], device_id=(facing, across), device_id_type=MESH,
            ).wait_recv()
            cross_copy(number, 1 - plane).start()

    def third(number):
        @pl.when(lax.rem(source(number), 2) != column)
        def _():
            cross_copy(number, plane).wait_recv()
            sibling_copy(number, core).start()

    cut = HALF // 2 // chips

    def cut_rows(plane_of, chip_of):
        start = core * HALF + plane_of * (HALF // 2) + chip_of * cut
        return pl.ds(pl.multiple_of(start, 16), cut)

    def cut_copy(n):
        if n < 4:
            seg_to, lon_to, rows = seg + 2 * n, me, cut_rows(plane, chip)
        else:
            seg_to, lon_to, rows = facing + 2 * n, across, cut_rows(1 - plane, chip)
        ref = other.at[0] if n % 2 else packs.at[seg]
        return pltpu.make_async_remote_copy(
            ref.at[rows], packs.at[seg, rows], a_send.at[n], a_recv.at[jnp.minimum(seg, EARLY - 1)],
            device_id=(lax.rem(seg_to, SEGS), lon_to), device_id_type=MESH,
        )

    def send_cuts():
        for n in (4, 1, 3, 5, 7, 2, 6):
            cut_copy(n).start()

    def spread_copy(number, n):
        rows = cut_rows(plane, chip)
        return pltpu.make_async_remote_copy(
            packs.at[number, rows], packs.at[number, rows], b_send.at[number, n], b_recv.at[number],
            device_id=(seg, on_chip(n)), device_id_type=MESH,
        )

    def spread(number):
        @pl.when(seg != number)
        def _():
            rows = cut_rows(plane, chip)
            pltpu.make_async_remote_copy(
                packs.at[number, rows], packs.at[number, rows], a_send.at[0], a_recv.at[number],
                device_id=(seg, across), device_id_type=MESH,
            ).wait_recv()
            for n in (1, chips - 1, 2, chips - 2, 3, chips - 3, 4):
                if 0 < n < chips:
                    spread_copy(number, n).start()

    def cross(number):
        @pl.when(seg != number)
        def _():
            start = core * HALF + plane * (HALF // 2)
            rows = pl.ds(pl.multiple_of(start, 16), HALF // 2 - cut)
            if chips > 1:
                pltpu.make_async_remote_copy(
                    packs.at[number, rows], packs.at[number, rows], b_send.at[number, 0],
                    b_recv.at[number], device_id=(seg, across), device_id_type=MESH,
                ).wait_recv()
            cross_copy(number, plane).start()

    def pair_up(number):
        @pl.when(seg != number)
        def _():
            cross_copy(number, 1 - plane).wait_recv()
            sibling_copy(number, core).start()

    def halo_copy(number, way):
        return pltpu.make_async_remote_copy(
            hist.at[number, pl.ds(TOK, TOK)],
            hist.at[number, pl.ds(2 * TOK if way == 0 else 0, TOK)],
            h_send.at[number, way],
            h_recv.at[number, way],
            device_id=(seg, west if way == 0 else east),
            device_id_type=MESH,
        )

    swap_copy = pltpu.make_async_remote_copy(
        swap, hist.at[0, pl.ds(TOK, TOK)], swap_sem.at[0], swap_sem.at[1],
        device_id=(seg, place), device_id_type=MESH,
    )

    prepare(0)
    stage[...] = jnp.zeros_like(stage)
    micro = order_ref[slot]
    for n in range(12):
        stage[12 * n : 12 * n + 12, :WIDTH] = fields_ref[micro, n // 6, lat, n % 6].astype(F32)

    pl.semaphore_wait(barrier, 14 + chips + 3)

    @pl.when(seg < EARLY)
    def _():
        send_cuts()

    @pl.when(seg >= EARLY)
    def _():
        send_weights(0)


    @pl.when(folded)
    def _():
        swap[...] = stage[...].astype(BF)
        swap_copy.start()
        swap_copy.wait_recv()

    @pl.when(jnp.logical_not(folded))
    def _():
        hist[0, TOK : 2 * TOK] = stage[...].astype(BF)

    for way in range(2):
        halo_copy(0, way).start()
    token = lax.broadcasted_iota(jnp.int32, (TOK, 128), 0)
    lon_ref[...] = lax.rem(token, LON).astype(F32)
    spread(0)
    prepare(1)
    cross(0)
    spread(1)
    pair_up(0)

    def params(number):
        return packs[number, PARAMS : PARAMS + 16, :].astype(F32)

    def offset(tile):
        row = lax.broadcasted_iota(jnp.int32, (16, 128), 0)
        return jnp.sum(jnp.where(row == 12 + slot, tile, 0.0), axis=0, keepdims=True)

    def step(number, decoder):
        if not decoder:
            @pl.when(number == 0)
            def _():
                @pl.when(seg >= SEGS // 2)
                def _():
                    send_weights(1)

                cross(1)
                spread(2)

            @pl.when(number == 1)
            def _():
                pair_up(1)
                for n in range(EARLY, 7):
                    first(n)
                cross(2)

            @pl.when(number == 2)
            def _():
                @pl.when(seg < SEGS // 2)
                def _():
                    send_weights(1)

                pair_up(2)
                for n in range(EARLY, 6):
                    second(n)

            @pl.when(number == 3)
            def _():
                third(3)
                third(4)

        @pl.when((number >= 2) & (number < SECTIONS - 5))
        def _():
            first(number + 5)

        @pl.when((number >= 3) & (number < SECTIONS - 3))
        def _():
            second(number + 3)

        @pl.when((number >= 4) & (number < SECTIONS - 1))
        def _():
            third(number + 1)

        @pl.when(source(number) != seg)
        def _():
            sibling_copy(number, 1 - core).wait_recv()

        tile = params(number)
        now = offset(tile)
        if decoder:
            before = offset(params(number - 1))
            aside = dot(pick(lon_ref[...], now - offset(params(15 - number))), hist[16 - number])
        else:
            before = offset(params(jnp.maximum(number - 1, 0)))
            before = before * jnp.where(number > 0, 1.0, 0.0)
        chosen = pick(lon_ref[...], now - before)
        for way in range(2):
            halo_copy(number, way).wait_recv()
        u = dot(chosen, hist[number])
        if decoder:
            u = ((u + aside) * 0.5).astype(BF).astype(F32)
        gain_a = side([tile[0:1] + tile[2:3] + tile[4:5], tile[1:2] + tile[3:4] + tile[5:6]])
        gain_b = side([tile[6:7] + tile[8:9] + tile[10:11], tile[7:8] + tile[9:10] + tile[11:12]])

        def strip(j):
            start = STRIP * j if j < 9 else HALF + STRIP * (j - 9)
            return packs[number, start : start + STRIP, :]

        def bias(j):
            start = HALF_W + TOK * j if j < 4 else HALF + HALF_W + TOK * (j - 4)
            return packs[number, start : start + TOK, :]

        hist[number + 1, TOK : 2 * TOK] = section(u, strip, bias, gain_a, gain_b)
        for way in range(2):
            halo_copy(number + 1, way).start()

    lax.fori_loop(0, 9, lambda i, c: (step(i, False), c)[1], 0)
    lax.fori_loop(9, SECTIONS, lambda i, c: (step(i, True), c)[1], 0)

    back = pick(lon_ref[...], -offset(params(SECTIONS - 1)))
    for way in range(2):
        halo_copy(SECTIONS, way).wait_recv()
    final = dot(back, hist[SECTIONS])
    share = WIDTH // SEGS
    for s in range(SEGS):
        pieces[s, :, :share] = final[:, share * s : share * (s + 1)].astype(BF)

    def piece_copy(d):
        there = lax.rem(seg + d, SEGS)
        return pltpu.make_async_remote_copy(
            pieces.at[there],
            received.at[seg],
            f_send.at[d],
            f_recv.at[d],
            device_id=(there, place),
            device_id_type=MESH,
        )

    for d in range(1, SEGS):
        piece_copy(d).start()
    mine = pltpu.make_async_copy(pieces.at[seg], received.at[seg], local_sem.at[0])

    @pl.when(folded)
    def _():
        piece_copy(0).start()

    @pl.when(jnp.logical_not(folded))
    def _():
        mine.start()

    def sent(half):
        for n in (1, 2, 3):
            own_copy(half, n).wait_send()

    sent(1)

    @pl.when(seg >= EARLY)
    def _():
        sent(0)

    @pl.when(seg < EARLY)
    def _():
        for n in range(1, SEGS):
            cut_copy(n).wait_send()

    def early_sent(number, carry):
        @pl.when(seg != number)
        def _():
            for n in range(1, chips):
                spread_copy(number, n).wait_send()
            cross_copy(number, plane).wait_send()

        return carry

    def late_sent(number, carry):
        same = lax.rem(source(number), 2) == column

        @pl.when(same)
        def _():
            facing_copy(number).wait_send()

        @pl.when(jnp.logical_not(same))
        def _():
            cross_copy(number, 1 - plane).wait_send()

        return carry

    lax.fori_loop(0, EARLY, early_sent, 0)
    lax.fori_loop(EARLY, SECTIONS, late_sent, 0)

    @pl.when(folded)
    def _():
        swap_copy.wait_send()

    def finish(number, carry):
        @pl.when((number < SECTIONS) & (source(number) != seg))
        def _():
            sibling_copy(number, core).wait_send()

        for way in range(2):
            halo_copy(number, way).wait_send()
        return carry

    lax.fori_loop(0, SECTIONS + 1, finish, 0)
    for d in range(1, SEGS):
        piece_copy(d).wait()

    @pl.when(folded)
    def _():
        piece_copy(0).wait()

    @pl.when(jnp.logical_not(folded))
    def _():
        mine.wait()

    out_ref[...] = received[...]


def split3(x):
    high = x.astype(BF).astype(F32)
    middle = (x - high).astype(BF).astype(F32)
    return high, middle, x - high - middle


def per_device(
    fields, entry_order, shift_offsets, qkv_weight, out_weight, up_weight, down_weight,
    attn_bias, norm_gain,
):
    dma = pltpu.SemaphoreType.DMA
    vmem = pl.BlockSpec(memory_space=pltpu.VMEM)
    smem = pl.BlockSpec(memory_space=pltpu.SMEM)
    got = pl.pallas_call(
        kernel,
        out_shape=jax.ShapeDtypeStruct((SEGS, TOK, 128), BF),
        in_specs=[vmem, smem, smem, vmem, vmem, vmem, vmem, vmem, vmem],
        out_specs=vmem,
        scratch_shapes=[
            pltpu.VMEM((SECTIONS, PACK, 128), BF),
            pltpu.VMEM((2, PACK, 128), BF),
            pltpu.VMEM((SECTIONS + 1, 3 * TOK, 256), BF),
            pltpu.VMEM((TOK, 128), F32),
            pltpu.VMEM((TOK, 256), F32),
            pltpu.VMEM((TOK, 256), BF),
            pltpu.VMEM((8, 256), F32),
            pltpu.VMEM((SEGS, TOK, 128), BF),
            pltpu.VMEM((SEGS, TOK, 128), BF),
            dma((1,)), dma((2,)), dma((SEGS,)), dma((EARLY,)), dma((EARLY, 8)), dma((EARLY,)),
            dma((SECTIONS,)), dma((SECTIONS,)), dma((SECTIONS,)), dma((SECTIONS,)), dma((2, 4)),
            dma((SECTIONS,)), dma((SECTIONS,)), dma((SECTIONS,)), dma((SECTIONS + 1, 2)), dma((SECTIONS + 1, 2)), dma((SEGS,)),
            dma((SEGS,)),
        ],
        compiler_params=pltpu.CompilerParams(
            collective_id=0, has_side_effects=True, vmem_limit_bytes=56 * 2**20
        ),
        name="sections",
    )(
        fields.reshape(4, 2, 2, 6, LON, WIDTH), entry_order, shift_offsets[:, :, 0],
        qkv_weight[:, 0], out_weight[:, 0], up_weight[:, 0], down_weight[:, 0],
        attn_bias[:, 0], norm_gain[:, 0],
    )
    share = WIDTH // SEGS
    got = got[:, :, :share].reshape(2, 2, 2, 2, 6, LON, share).transpose(0, 2, 3, 1, 4, 5, 6)
    got = got.reshape(4, 2, 12, LON, share)
    chosen = (entry_order[None, :] == jnp.arange(4)[:, None]).astype(jnp.int32)
    place = jnp.sum(chosen * jnp.arange(4)[None, :], axis=1)
    return jnp.take(got, place, axis=0)


def solution(mesh):
    placed = (
        P(None, None, None, "lon", None),
        P(),
        P(None, None, "segment"),
        P(None, "segment", None, None),
        P(None, "segment", None, None),
        P(None, "segment", None, None),
        P(None, "segment", None, None),
        P(None, "segment", None, None, None, None),
        P(None, "segment", None, None),
    )
    return jax.shard_map(
        per_device,
        mesh=mesh,
        in_specs=placed,
        out_specs=P(None, None, None, "lon", "segment"),
        check_vma=False,
    )
```

time: 230 us -> 162 us (0.70)
  Pallas kernels: 179 us -> 150 us
  local copies, waits for them, and re-layouts: 35 us -> 8.13 us
  other arithmetic: 12.3 us -> 1.18 us
  between operations: 2.61 us -> 0.05 us
    pallas_call x1, Pallas kernels: 179 us -> 150 us  [per_device(): pl.pallas_call(kernel, out_shape=jax.ShapeDtypeStruct((SEGS, TOK, 128), B...]
    unnamed x41 -> x4, local copies, waits for them, and re-layouts: 15.9 us -> 4.31 us
    another operation x23 -> x0, local copies, waits for them, and re-layouts: 5.92 us -> none  [the longest x22 5.12 us: pack_weights(): small = jnp.stack(rows)]
    concatenate x8 -> x0, other arithmetic: 5.08 us -> none  [the longest x2 3.51 us: pack_weights(): own = jnp.concatenate([weights, here], axis=1).reshape(PACK, 128)]
    reduce_max x1 -> x0, other arithmetic: 3.04 us -> none  [pack_weights(): top = jnp.max(bias, axis=-1, keepdims=True)]
    dynamic_slice x5 -> x0, local copies, waits for them, and re-layouts: 2.82 us -> none  [the longest x2 1.52 us: pack_weights(): there = lax.dynamic_index_in_dim(bias, 1 - lat, 0, keepdims=False)]
    reshape x3 -> x0, local copies, waits for them, and re-layouts: 2.81 us -> none  [the longest x1 1.57 us: per_device(): x = jnp.pad(grid.reshape(TOK, WIDTH), ((0, 0), (0, 64)))]
    slice x34 -> x1, local copies, waits for them, and re-layouts: 3.62 us -> 1.04 us  [per_device(): got[:, :, :share].reshape(2, 2, 2, 2, 6, LON, share)]
where the time goes in v2:
time: 162 us; the launch traced here: 159 us
  Pallas kernels  150 us (93%)
  local copies, waits for them, and re-layouts  8.13 us (5%)
    pallas_call x1, Pallas kernels, per_device(): pl.pallas_call(kernel, out_shape=jax.ShapeDtypeStruct((SEGS, TOK, 128), B...  150 us
    unnamed x4, local copies, waits for them, and re-layouts  4.31 us

profile of v2, /device:TPU:4, one launch (start us, length us, event | category | flops | bytes accessed | tf_op | source)
XLA Modules:
  0.0 159.2 jit_solution(2445602360051529269)
XLA Ops:
  0.0 2.1 %copy.18 = bf16[4,2,12,12,192]{4,3,2,1,0:T(8,128)(2,1)} copy(bf16[4,2,12,12,192]{4,1,3,2,0:T(2,128)(2,1)} %param.9) | data formatting | bytes 884736 | tf_op args[0]
  2.1 1.3 copy.20.shift_ref
  3.4 2.2 %copy.19 = bf16[2,1,768,192]{3,2,0,1:T(8,128)(2,1)} copy(bf16[2,1,768,192]{2,3,1,0:T(8,128)(2,1)} %param.15) | data formatting | bytes 1179648 | tf_op args[6]
  5.6 0.0 copy-start
  5.6 149.9 %sections.1 = bf16[8,144,128]{2,1,0:T(8,128)(2,1)} custom-call(bf16[4,2,2,6,12,192]{5,4,3,2,1,0:T(8,128)(2,1)} %bitcast.18, s32[4]{0:T(128)} %order_ref.1, s32[4,2]{1,0:T(4,128)} %copy.20.shift_ref, bf16[2,192,576]{2,1,0:T(8,128)(2,1)} %bitcast.24, bf16[2,192,192]{2,1,0:T(8,128)(2,1)} %bitcast.25, bf16[2,192,768]{2,1,0:T(8,128)(2,1)} %bitcast.23, ...), custom_call_target="tpu_custom_call" | custom-call | tf_op jit(solution)/shard_map/sections/pallas_call | solution.py:613
  155.5 1.0 copy.21
  156.5 0.3 copy.22
  156.9 0.0 copy-done
  156.9 0.1 select_reduce_fusion
  157.0 1.1 gather_fusion
  158.2 1.0 broadcast_select_fusion
  (3 shorter events, 0.0 us)
Async XLA Ops:
  5.6 151.2 %copy-start = (s32[4]{0:T(128)S(1)}, s32[4]{0:T(128)}, u32[]{:S(2)}) copy-start(s32[4]{0:T(128)} %order_ref.1) | copy-start | bytes 52

commit v3 on v2

--- a/solution.py
+++ b/solution.py
@@ -55,11 +55,10 @@
     return (centred * lax.rsqrt(spread + EPS) * gain).astype(BF)
 
 
-def pick(lon, shift):
-    row = lax.broadcasted_iota(jnp.int32, (TOK, 128), 0).astype(F32)
+def pick(token, lon, shift):
     x = lon + shift
     wrap = jnp.where(x < 0, float(LON - TOK), jnp.where(x > LON - 1, float(TOK - LON), 0.0))
-    target = row + shift + wrap + float(TOK)
+    target = token + shift + wrap + float(TOK)
     col = lanes((TOK, 128)).astype(F32)
     tiles = [jnp.where(col + float(128 * j) == target, 1.0, 0.0).astype(BF) for j in range(4)]
     return side(tiles)[:, : 3 * TOK]
@@ -100,17 +99,15 @@
     x1 = u + out.astype(BF).astype(F32)
     normed = normalize(x1, gain_b, inside)[:, :WIDTH]
     hidden = jax.nn.gelu(dot(normed, side([strip(6 + j) for j in range(6)]))).astype(BF)
-    tail = down([strip(16), strip(17)])
-    y0 = dot(hidden[:, :384], side([down([strip(12), strip(13)]), tail]))
-    y1 = dot(hidden[:, 384:], side([down([strip(14), strip(15)]), tail]))
-    y = side([y0[:, :128] + y1[:, :128], (y0[:, 128:] + pltpu.roll(y1[:, 128:], 64, 1)) * low])
+    low_t = down([side([strip(12 + j) for j in range(6)]), jnp.zeros((64, 768), BF)])
+    y = dot(hidden, low_t, NT)
     return (x1 + y).astype(BF)
 
 
 def kernel(
     fields_ref, order_ref, shift_ref, qkv_ref, out_w_ref, up_ref, low_ref, bias_ref, gain_ref,
     out_ref,
-    packs, other, hist, lon_ref, stage, swap, gains, pieces, received,
+    packs, other, hist, token_ref, lon_ref, stage, swap, gains, pieces, received,
     local_sem, swap_sem, a_send, a_recv, b_send, b_recv, x_send, x_recv,
     c_send, c_recv, w_send, w_recv, s_send, s_recv, h_send, h_recv, f_send, f_recv,
 ):
@@ -190,12 +187,7 @@
         put_strip(5, out_w[:, :128])
         for j in range(6):
             put_strip(6 + j, up_ref[half, :, 128 * j : 128 * j + 128])
-        for j in range(4):
-            put_strip(12 + j, low_ref[half, STRIP * j : STRIP * j + STRIP, :128])
-        for j in range(2):
-            upper = low_ref[half, STRIP * j : STRIP * j + STRIP, 128:].astype(F32)
-            lower = low_ref[half, 384 + STRIP * j : 384 + STRIP * j + STRIP, 128:].astype(F32)
-            put_strip(16 + j, side([upper, lower]))
+            put_strip(12 + j, low_ref[half, :, 128 * j : 128 * j + 128])
 
         eye = (lax.broadcasted_iota(jnp.int32, (TOK, TOK), 0) == lanes((TOK, TOK)))
         eye = jnp.where(eye, 1.0, 0.0).astype(BF)
@@ -223,7 +215,7 @@
         for n in range(2):
             for part in split3(gains[n : n + 1, :]):
                 rows += [part[:, :128], part[:, 128:]]
-        rows += [jnp.full((1, 128), shift_ref[t, half].astype(F32)) for t in range(4)]
+        rows += [jnp.full((1, 128), shift_ref[half, 0, t].astype(F32)) for t in range(4)]
         put(PARAMS, down(rows))
         rest = jnp.zeros((TOK - 16, 128), BF)
         put(PARAMS + 16, rest)
@@ -306,20 +298,26 @@
         start = core * HALF + plane_of * (HALF // 2) + chip_of * cut
         return pl.ds(pl.multiple_of(start, 16), cut)
 
-    def cut_copy(n):
+    far = chips // 2
+
+    def cut_copy(n, k):
+        of = lax.rem(chip + k * far, chips)
         if n < 4:
-            seg_to, lon_to, rows = seg + 2 * n, me, cut_rows(plane, chip)
+            seg_to, lon_to, rows = seg + 2 * n, me, cut_rows(plane, of)
         else:
-            seg_to, lon_to, rows = facing + 2 * n, across, cut_rows(1 - plane, chip)
+            seg_to, lon_to, rows = facing + 2 * n, across, cut_rows(1 - plane, of)
         ref = other.at[0] if n % 2 else packs.at[seg]
         return pltpu.make_async_remote_copy(
-            ref.at[rows], packs.at[seg, rows], a_send.at[n], a_recv.at[jnp.minimum(seg, EARLY - 1)],
+            ref.at[rows], packs.at[seg, rows], a_send.at[n, k], a_recv.at[jnp.minimum(seg, EARLY - 1)],
             device_id=(lax.rem(seg_to, SEGS), lon_to), device_id_type=MESH,
         )
 
     def send_cuts():
         for n in (4, 1, 3, 5, 7, 2, 6):
-            cut_copy(n).start()
+            for k in range(2 if chips > 1 else 1):
+                cut_copy(n, k).start()
+
+    peers = [n for k in range(1, far) for n in (k, chips - k)]
 
     def spread_copy(number, n):
         rows = cut_rows(plane, chip)
@@ -331,20 +329,19 @@
     def spread(number):
         @pl.when(seg != number)
         def _():
-            rows = cut_rows(plane, chip)
+            rows = pl.ds(pl.multiple_of(core * HALF, 16), cut * (2 if chips > 1 else 1))
             pltpu.make_async_remote_copy(
-                packs.at[number, rows], packs.at[number, rows], a_send.at[0], a_recv.at[number],
+                packs.at[number, rows], packs.at[number, rows], a_send.at[0, 0], a_recv.at[number],
                 device_id=(seg, across), device_id_type=MESH,
             ).wait_recv()
-            for n in (1, chips - 1, 2, chips - 2, 3, chips - 3, 4):
-                if 0 < n < chips:
-                    spread_copy(number, n).start()
+            for n in peers:
+                spread_copy(number, n).start()
 
     def cross(number):
         @pl.when(seg != number)
         def _():
             start = core * HALF + plane * (HALF // 2)
-            rows = pl.ds(pl.multiple_of(start, 16), HALF // 2 - cut)
+            rows = pl.ds(pl.multiple_of(start, 16), max(1, len(peers)) * cut)
             if chips > 1:
                 pltpu.make_async_remote_copy(
                     packs.at[number, rows], packs.at[number, rows], b_send.at[number, 0],
@@ -376,8 +373,11 @@
     prepare(0)
     stage[...] = jnp.zeros_like(stage)
     micro = order_ref[slot]
-    for n in range(12):
-        stage[12 * n : 12 * n + 12, :WIDTH] = fields_ref[micro, n // 6, lat, n % 6].astype(F32)
+    for n in range(6):
+        cells = fields_ref[micro, 6 * lat + n].astype(F32)
+        for level in range(2):
+            start = 72 * level + LON * n
+            stage[start : start + LON, :WIDTH] = cells[:, level, :]
 
     pl.semaphore_wait(barrier, 14 + chips + 3)
 
@@ -403,11 +403,14 @@
     for way in range(2):
         halo_copy(0, way).start()
     token = lax.broadcasted_iota(jnp.int32, (TOK, 128), 0)
+    token_ref[...] = token.astype(F32)
     lon_ref[...] = lax.rem(token, LON).astype(F32)
     spread(0)
     prepare(1)
     cross(0)
     spread(1)
+    cross(1)
+    spread(2)
     pair_up(0)
 
     def params(number):
@@ -425,9 +428,6 @@
                 def _():
                     send_weights(1)
 
-                cross(1)
-                spread(2)
-
             @pl.when(number == 1)
             def _():
                 pair_up(1)
@@ -470,11 +470,12 @@
         now = offset(tile)
         if decoder:
             before = offset(params(number - 1))
-            aside = dot(pick(lon_ref[...], now - offset(params(15 - number))), hist[16 - number])
+            earlier = now - offset(params(15 - number))
+            aside = dot(pick(token_ref[...], lon_ref[...], earlier), hist[16 - number])
         else:
             before = offset(params(jnp.maximum(number - 1, 0)))
             before = before * jnp.where(number > 0, 1.0, 0.0)
-        chosen = pick(lon_ref[...], now - before)
+        chosen = pick(token_ref[...], lon_ref[...], now - before)
         for way in range(2):
             halo_copy(number, way).wait_recv()
         u = dot(chosen, hist[number])
@@ -498,7 +499,10 @@
     lax.fori_loop(0, 9, lambda i, c: (step(i, False), c)[1], 0)
     lax.fori_loop(9, SECTIONS, lambda i, c: (step(i, True), c)[1], 0)
 
-    back = pick(lon_ref[...], -offset(params(SECTIONS - 1)))
+    order = lax.broadcasted_iota(jnp.int32, (TOK, 128), 0)
+    lon = lax.rem(order, 24) // 2
+    token = (lax.rem(order, 2) * 6 + order // 24) * LON + lon
+    back = pick(token.astype(F32), lon.astype(F32), -offset(params(SECTIONS - 1)))
     for way in range(2):
         halo_copy(SECTIONS, way).wait_recv()
     final = dot(back, hist[SECTIONS])
@@ -542,12 +546,13 @@
     @pl.when(seg < EARLY)
     def _():
         for n in range(1, SEGS):
-            cut_copy(n).wait_send()
+            for k in range(2 if chips > 1 else 1):
+                cut_copy(n, k).wait_send()
 
     def early_sent(number, carry):
         @pl.when(seg != number)
         def _():
-            for n in range(1, chips):
+            for n in peers:
                 spread_copy(number, n).wait_send()
             cross_copy(number, plane).wait_send()
 
@@ -594,7 +599,12 @@
     def _():
         mine.wait()
 
-    out_ref[...] = received[...]
+    for m in range(4):
+        at = jnp.int32(0)
+        for t in range(1, 4):
+            at = jnp.where(order_ref[t] == m, 4 * (t // 2) + t % 2, at)
+        for a in range(2):
+            out_ref[m, a] = received[at + 2 * a]
 
 
 def split3(x):
@@ -612,7 +622,7 @@
     smem = pl.BlockSpec(memory_space=pltpu.SMEM)
     got = pl.pallas_call(
         kernel,
-        out_shape=jax.ShapeDtypeStruct((SEGS, TOK, 128), BF),
+        out_shape=jax.ShapeDtypeStruct((4, 2, TOK, 128), BF),
         in_specs=[vmem, smem, smem, vmem, vmem, vmem, vmem, vmem, vmem],
         out_specs=vmem,
         scratch_shapes=[
@@ -620,12 +630,13 @@
             pltpu.VMEM((2, PACK, 128), BF),
             pltpu.VMEM((SECTIONS + 1, 3 * TOK, 256), BF),
             pltpu.VMEM((TOK, 128), F32),
+            pltpu.VMEM((TOK, 128), F32),
             pltpu.VMEM((TOK, 256), F32),
             pltpu.VMEM((TOK, 256), BF),
             pltpu.VMEM((8, 256), F32),
             pltpu.VMEM((SEGS, TOK, 128), BF),
             pltpu.VMEM((SEGS, TOK, 128), BF),
-            dma((1,)), dma((2,)), dma((SEGS,)), dma((EARLY,)), dma((EARLY, 8)), dma((EARLY,)),
+            dma((1,)), dma((2,)), dma((SEGS, 2)), dma((EARLY,)), dma((EARLY, 8)), dma((EARLY,)),
             dma((SECTIONS,)), dma((SECTIONS,)), dma((SECTIONS,)), dma((SECTIONS,)), dma((2, 4)),
             dma((SECTIONS,)), dma((SECTIONS,)), dma((SECTIONS,)), dma((SECTIONS + 1, 2)), dma((SECTIONS + 1, 2)), dma((SEGS,)),
             dma((SEGS,)),
@@ -635,16 +646,13 @@
         ),
         name="sections",
     )(
-        fields.reshape(4, 2, 2, 6, LON, WIDTH), entry_order, shift_offsets[:, :, 0],
-        qkv_weight[:, 0], out_weight[:, 0], up_weight[:, 0], down_weight[:, 0],
+        fields.transpose(0, 2, 3, 1, 4), entry_order, shift_offsets.transpose(1, 2, 0),
+        qkv_weight[:, 0], out_weight[:, 0], up_weight[:, 0], down_weight[:, 0].swapaxes(1, 2),
         attn_bias[:, 0], norm_gain[:, 0],
     )
     share = WIDTH // SEGS
-    got = got[:, :, :share].reshape(2, 2, 2, 2, 6, LON, share).transpose(0, 2, 3, 1, 4, 5, 6)
-    got = got.reshape(4, 2, 12, LON, share)
-    chosen = (entry_order[None, :] == jnp.arange(4)[:, None]).astype(jnp.int32)
-    place = jnp.sum(chosen * jnp.arange(4)[None, :], axis=1)
-    return jnp.take(got, place, axis=0)
+    got = got[..., :share].reshape(4, 12, LON, 2, share)
+    return got.transpose(0, 3, 1, 2, 4)
 
 
 def solution(mesh):

time: 162 us -> 151 us (0.932)
  local copies, waits for them, and re-layouts: 8.13 us -> 1.88 us
  Pallas kernels: 150 us -> 146 us
    pallas_call x1, Pallas kernels: 150 us -> 146 us  [per_device(): pl.pallas_call(kernel, out_shape=jax.ShapeDtypeStruct((4, 2, TOK, 128), B...]
    unnamed x4 -> x1, local copies, waits for them, and re-layouts: 4.31 us -> 1.88 us
where the time goes in v3:
time: 151 us; the launch traced here: 148 us
  Pallas kernels  146 us (97%)
  local copies, waits for them, and re-layouts  1.88 us (1%)
    pallas_call x1, Pallas kernels, per_device(): pl.pallas_call(kernel, out_shape=jax.ShapeDtypeStruct((4, 2, TOK, 128), B...  146 us

profile of v3, /device:TPU:4, one launch (start us, length us, event | category | flops | bytes accessed | tf_op | source)
XLA Modules:
  0.0 147.7 jit_solution(11685082839620372464)
XLA Ops:
  0.0 145.8 %sections.1 = bf16[4,2,144,128]{3,2,1,0:T(8,128)(2,1)} custom-call(bf16[4,12,12,2,192]{4,3,2,1,0:T(2,128)(2,1)} %bitcast.16, s32[4]{0:T(128)} %order_ref.1, s32[2,1,4]{2,1,0:T(1,128)} %bitcast.22, bf16[2,192,576]{2,1,0:T(8,128)(2,1)} %bitcast.19, bf16[2,192,192]{2,1,0:T(8,128)(2,1)} %bitcast.20, bf16[2,192,768]{2,1,0:T(8,128)(2,1)} %bitcast.17, ...), custom_call_target="tpu_custom_call" | custom-call | tf_op jit(solution)/shard_map/sections/pallas_call | solution.py:623
  145.8 1.9 %copy.11 = bf16[4,2,12,12,24]{4,1,3,2,0:T(2,128)(2,1)} copy(bf16[4,2,12,12,24]{4,1,3,2,0:T(2,128)(2,1)} %bitcast.15) | data formatting | bytes 110592

commit v4 on v3

--- a/solution.py
+++ b/solution.py
@@ -27,6 +27,7 @@
 HALF_B = 4 * TOK
 HALF = HALF_W + HALF_B
 PACK = 2 * HALF
+ROWS = TOK // 3
 PARAMS = HALF + HALF_W + 3 * TOK
 EPS = 1e-5
 QSCALE = math.log2(math.e) / math.sqrt(32.0)
@@ -105,12 +106,16 @@
 
 
 def kernel(
-    fields_ref, order_ref, shift_ref, qkv_ref, out_w_ref, up_ref, low_ref, bias_ref, gain_ref,
-    out_ref,
-    packs, other, hist, token_ref, lon_ref, stage, swap, gains, pieces, received,
-    local_sem, swap_sem, a_send, a_recv, b_send, b_recv, x_send, x_recv,
-    c_send, c_recv, w_send, w_recv, s_send, s_recv, h_send, h_recv, f_send, f_recv,
+    order_ref, shift_ref, gain_ref, *refs,
 ):
+    given, out_ref, held, rest = refs[:6], refs[6], refs[7:13], refs[13:]
+    fields_ref, qkv_ref, out_w_ref, up_ref, low_ref, bias_ref = held
+    (
+        packs, other, hist, token_ref, lon_ref, share_ref, stage, swap, gains, pieces, received,
+        local_sem, swap_sem, a_send, a_recv, b_send, b_recv, x_send, x_recv,
+        c_send, c_recv, w_send, w_recv, s_send, s_recv, h_send, h_recv, f_send, f_recv,
+        in_sem,
+    ) = rest
     seg = lax.axis_index("segment")
     me = lax.axis_index("lon")
     ring = lax.axis_size("lon")
@@ -131,6 +136,11 @@
     place = along(me)
     west, east = along(place - 1), along(place + 1)
 
+    def arrival(n, half):
+        if n == 0:
+            return pltpu.make_async_copy(given[0], held[0], in_sem.at[n, half])
+        return pltpu.make_async_copy(given[n].at[half], held[n].at[half], in_sem.at[n, half])
+
     barrier = pltpu.get_barrier_semaphore()
 
     def greet(seg_to, lon_to):
@@ -157,6 +167,11 @@
     for n in range(1, 4):
         greet(lax.rem(facing + 2 * n, SEGS), across)
 
+    for n in (5, 1, 2, 3, 4, 0):
+        arrival(n, 0).start()
+    for n in range(1, 6):
+        arrival(n, 1).start()
+
     def source(number):
         return jnp.minimum(number, SECTIONS - 1 - number)
 
@@ -165,6 +180,8 @@
 
     def prepare(half):
         number = own_number(half)
+        for n in range(1, 6):
+            arrival(n, half).wait()
 
         def put(start, block):
             block = block.astype(BF)
@@ -372,6 +389,7 @@
 
     prepare(0)
     stage[...] = jnp.zeros_like(stage)
+    arrival(0, 0).wait()
     micro = order_ref[slot]
     for n in range(6):
         cells = fields_ref[micro, 6 * lat + n].astype(F32)
@@ -404,6 +422,16 @@
         halo_copy(0, way).start()
     token = lax.broadcasted_iota(jnp.int32, (TOK, 128), 0)
     token_ref[...] = token.astype(F32)
+    share = WIDTH // SEGS
+    feature = lax.broadcasted_iota(jnp.int32, (256, 128), 0)
+    for g in range(3):
+        lane = lanes((256, 128)) - 32 * g
+        inside = (lane >= 0) & (lane < share)
+        for s in range(SEGS):
+            hit = inside & (feature == lane + share * s)
+            share_ref[256 * g : 256 * g + 256, 128 * s : 128 * s + 128] = jnp.where(
+                hit, 1.0, 0.0
+            ).astype(BF)
     lon_ref[...] = lax.rem(token, LON).astype(F32)
     spread(0)
     prepare(1)
@@ -505,10 +533,11 @@
     back = pick(token.astype(F32), lon.astype(F32), -offset(params(SECTIONS - 1)))
     for way in range(2):
         halo_copy(SECTIONS, way).wait_recv()
-    final = dot(back, hist[SECTIONS])
-    share = WIDTH // SEGS
+    final = dot(back, hist[SECTIONS]).astype(BF)
+    final = side([final[ROWS * g : ROWS * g + ROWS] for g in range(3)])
+    final = dot(final, share_ref[...]).astype(BF)
     for s in range(SEGS):
-        pieces[s, :, :share] = final[:, share * s : share * (s + 1)].astype(BF)
+        pieces[s] = final[:, 128 * s : 128 * s + 128]
 
     def piece_copy(d):
         there = lax.rem(seg + d, SEGS)
@@ -604,7 +633,10 @@
         for t in range(1, 4):
             at = jnp.where(order_ref[t] == m, 4 * (t // 2) + t % 2, at)
         for a in range(2):
-            out_ref[m, a] = received[at + 2 * a]
+            piece = received[at + 2 * a].astype(F32)
+            for g in range(3):
+                turned = pltpu.roll(piece, 128 - 32 * g, 1) if g else piece
+                out_ref[m, a, ROWS * g : ROWS * g + ROWS] = turned.astype(BF)
 
 
 def split3(x):
@@ -618,38 +650,39 @@
     attn_bias, norm_gain,
 ):
     dma = pltpu.SemaphoreType.DMA
+    stored = (
+        fields.transpose(0, 2, 3, 1, 4), qkv_weight[:, 0], out_weight[:, 0], up_weight[:, 0],
+        down_weight[:, 0].swapaxes(1, 2), attn_bias[:, 0],
+    )
     vmem = pl.BlockSpec(memory_space=pltpu.VMEM)
     smem = pl.BlockSpec(memory_space=pltpu.SMEM)
     got = pl.pallas_call(
         kernel,
         out_shape=jax.ShapeDtypeStruct((4, 2, TOK, 128), BF),
-        in_specs=[vmem, smem, smem, vmem, vmem, vmem, vmem, vmem, vmem],
+        in_specs=[smem, smem, vmem] + [pl.BlockSpec(memory_space=pl.ANY)] * 6,
         out_specs=vmem,
-        scratch_shapes=[
+        scratch_shapes=[pltpu.VMEM(a.shape, a.dtype) for a in stored] + [
             pltpu.VMEM((SECTIONS, PACK, 128), BF),
             pltpu.VMEM((2, PACK, 128), BF),
             pltpu.VMEM((SECTIONS + 1, 3 * TOK, 256), BF),
             pltpu.VMEM((TOK, 128), F32),
             pltpu.VMEM((TOK, 128), F32),
+            pltpu.VMEM((768, 1024), BF),
             pltpu.VMEM((TOK, 256), F32),
             pltpu.VMEM((TOK, 256), BF),
             pltpu.VMEM((8, 256), F32),
-            pltpu.VMEM((SEGS, TOK, 128), BF),
-            pltpu.VMEM((SEGS, TOK, 128), BF),
+            pltpu.VMEM((SEGS, ROWS, 128), BF),
+            pltpu.VMEM((SEGS, ROWS, 128), BF),
             dma((1,)), dma((2,)), dma((SEGS, 2)), dma((EARLY,)), dma((EARLY, 8)), dma((EARLY,)),
             dma((SECTIONS,)), dma((SECTIONS,)), dma((SECTIONS,)), dma((SECTIONS,)), dma((2, 4)),
             dma((SECTIONS,)), dma((SECTIONS,)), dma((SECTIONS,)), dma((SECTIONS + 1, 2)), dma((SECTIONS + 1, 2)), dma((SEGS,)),
-            dma((SEGS,)),
+            dma((SEGS,)), dma((6, 2)),
         ],
         compiler_params=pltpu.CompilerParams(
             collective_id=0, has_side_effects=True, vmem_limit_bytes=56 * 2**20
         ),
         name="sections",
-    )(
-        fields.transpose(0, 2, 3, 1, 4), entry_order, shift_offsets.transpose(1, 2, 0),
-        qkv_weight[:, 0], out_weight[:, 0], up_weight[:, 0], down_weight[:, 0].swapaxes(1, 2),
-        attn_bias[:, 0], norm_gain[:, 0],
-    )
+    )(entry_order, shift_offsets.transpose(1, 2, 0), norm_gain[:, 0], *stored)
     share = WIDTH // SEGS
     got = got[..., :share].reshape(4, 12, LON, 2, share)
     return got.transpose(0, 3, 1, 2, 4)

time: 151 us -> 146 us (0.967); the launches traced: 148 us -> 145 us
  Pallas kernels: 146 us -> 144 us
    pallas_call x1, Pallas kernels: 146 us -> 144 us  [per_device(): pl.pallas_call(kernel, out_shape=jax.ShapeDtypeStruct((4, 2, TOK, 128), B...]
where the time goes in v4:
time: 146 us; the launch traced here: 145 us
  Pallas kernels  144 us (99%)
  local copies, waits for them, and re-layouts  1.88 us (1%)
    pallas_call x1, Pallas kernels, per_device(): pl.pallas_call(kernel, out_shape=jax.ShapeDtypeStruct((4, 2, TOK, 128), B...  144 us

profile of v4, /device:TPU:4, one launch (start us, length us, event | category | flops | bytes accessed | tf_op | source)
XLA Modules:
  0.0 145.5 jit_solution(9494325288459535682)
XLA Ops:
  0.0 143.6 %sections.1 = bf16[4,2,144,128]{3,2,1,0:T(8,128)(2,1)} custom-call(s32[4]{0:T(128)} %order_ref.1, s32[2,1,4]{2,1,0:T(1,128)} %bitcast.22, f32[2,2,192]{2,1,0:T(2,128)} %bitcast.21, bf16[4,12,12,2,192]{4,3,2,1,0:T(2,128)(2,1)} %bitcast.16, bf16[2,192,576]{2,1,0:T(8,128)(2,1)} %bitcast.19, bf16[2,192,192]{2,1,0:T(8,128)(2,1)} %bitcast.20, ...), custom_call_target="tpu_custom_call" | custom-call | tf_op jit(solution)/shard_map/sections/pallas_call | solution.py:659
  143.6 1.9 %copy.11 = bf16[4,2,12,12,24]{4,1,3,2,0:T(2,128)(2,1)} copy(bf16[4,2,12,12,24]{4,1,3,2,0:T(2,128)(2,1)} %bitcast.15) | data formatting | bytes 110592

commit v5 on v4

--- a/solution.py
+++ b/solution.py
@@ -17,18 +17,21 @@
 
 SEGS = 8
 SECTIONS = 16
-EARLY = 3
+EARLY = 4
 HEADS = 6
 TOK = 144
 WIDTH = 192
 LON = 12
 STRIP = 192
-HALF_W = 9 * STRIP
-HALF_B = 4 * TOK
-HALF = HALF_W + HALF_B
-PACK = 2 * HALF
+BIAS = 6 * STRIP
+PARAMS = BIAS + 7 * TOK
+AFTER = BIAS + 8 * TOK
+PACK = AFTER + 12 * STRIP
+HALF = PACK // 2
+CHUNKS = ((0, 2560), (2560, 2048))
 ROWS = TOK // 3
-PARAMS = HALF + HALF_W + 3 * TOK
+FOLD = TOK // 2
+BAND = TOK + FOLD + 8
 EPS = 1e-5
 QSCALE = math.log2(math.e) / math.sqrt(32.0)
 
@@ -58,14 +61,41 @@
 
 def pick(token, lon, shift):
     x = lon + shift
-    wrap = jnp.where(x < 0, float(LON - TOK), jnp.where(x > LON - 1, float(TOK - LON), 0.0))
-    target = token + shift + wrap + float(TOK)
+    west, east = x < 0, x > LON - 1
+    block = jnp.where(west, 0.0, jnp.where(east, 2.0, 1.0))
+    of = token + shift + jnp.where(west, float(LON), jnp.where(east, float(-LON), 0.0))
+    upper = of >= FOLD
+    first = block * float(TOK) + of
+    second = block * float(BAND - TOK) + jnp.where(upper, of - float(FOLD), of)
     col = lanes((TOK, 128)).astype(F32)
-    tiles = [jnp.where(col + float(128 * j) == target, 1.0, 0.0).astype(BF) for j in range(4)]
-    return side(tiles)[:, : 3 * TOK]
-
-
-def section(u, strip, bias, gain_a, gain_b):
+
+    def hot(hit):
+        return jnp.where(hit, 1.0, 0.0).astype(BF)
+
+    take = side([hot(col + float(128 * j) == first) for j in range(4)])[:, : 3 * TOK]
+    hits = [col + float(128 * j) == second for j in range(2)]
+    rest = down(
+        [side([hot(hit & half) for hit in hits]) for half in (jnp.logical_not(upper), upper)]
+    )[:, : 3 * (BAND - TOK)]
+    return take, rest
+
+
+def taken(chosen, bands, at):
+    take, rest = chosen
+    starts = (0, BAND, 2 * BAND)
+    first = dot(take, down([bands[at, r : r + TOK, :] for r in starts]))
+    second = dot(rest, down([bands[at, r + TOK : r + BAND, :] for r in starts]))
+    low = jnp.where(lanes((1, 128)) < 64, 1.0, 0.0)
+    second = (second[:TOK] + pltpu.roll(second[TOK:], 64, 1)) * low
+    return side([first, second])
+
+
+def folded_band(h):
+    rest = h[:FOLD, 128:] + pltpu.roll(h[FOLD:, 128:], 64, 1)
+    return down([h[:, :128], rest, jnp.zeros((8, 128), F32)]).astype(BF)
+
+
+def section(u, strip, bias, gain_a, gain_b, ready=None):
     col = lanes((1, 256))
     inside = jnp.where(col < WIDTH, 1.0, 0.0)
     low = jnp.where(lanes((1, 128)) < 64, 1.0, 0.0)
@@ -99,10 +129,12 @@
     out = side([out[:, :128], pltpu.roll(out[:, 128:], 64, 1) * low])
     x1 = u + out.astype(BF).astype(F32)
     normed = normalize(x1, gain_b, inside)[:, :WIDTH]
+    if ready is not None:
+        ready()
     hidden = jax.nn.gelu(dot(normed, side([strip(6 + j) for j in range(6)]))).astype(BF)
     low_t = down([side([strip(12 + j) for j in range(6)]), jnp.zeros((64, 768), BF)])
     y = dot(hidden, low_t, NT)
-    return (x1 + y).astype(BF)
+    return x1 + y
 
 
 def kernel(
@@ -112,7 +144,8 @@
     fields_ref, qkv_ref, out_w_ref, up_ref, low_ref, bias_ref = held
     (
         packs, other, hist, token_ref, lon_ref, share_ref, stage, swap, gains, pieces, received,
-        local_sem, swap_sem, a_send, a_recv, b_send, b_recv, x_send, x_recv,
+        local_sem, swap_sem, a_send, a_recv, b_send, b_recv, e_send, e_recv, d_send,
+        d_recv, x_send, x_recv,
         c_send, c_recv, w_send, w_recv, s_send, s_recv, h_send, h_recv, f_send, f_recv,
         in_sem,
     ) = rest
@@ -189,7 +222,7 @@
             other[half, start : start + block.shape[0], :] = block
 
         def put_strip(j, block):
-            put(STRIP * j if j < 9 else HALF + STRIP * (j - 9), block)
+            put(STRIP * j if j < 6 else AFTER + STRIP * (j - 6), block)
 
         low = lanes((STRIP, 128)) < 64
         qkv = [qkv_ref[half, :, 128 * j : 128 * j + 128].astype(F32) for j in range(4)]
@@ -215,8 +248,7 @@
             table = ((table - top) * math.log2(math.e)).astype(BF)
             table = dot(eye, down([table, jnp.zeros((32, TOK), BF)]), NT).astype(BF)
             for j in range(7):
-                start = HALF_W + TOK * j if j < 4 else HALF + HALF_W + TOK * (j - 4)
-                store(start, table[:, 128 * j : 128 * j + 128])
+                store(BIAS + TOK * j, table[:, 128 * j : 128 * j + 128])
 
         def store_own(start, block):
             packs[number, start : start + TOK, :] = block
@@ -309,73 +341,94 @@
             cross_copy(number, plane).wait_recv()
             sibling_copy(number, core).start()
 
-    cut = HALF // 2 // chips
-
-    def cut_rows(plane_of, chip_of):
-        start = core * HALF + plane_of * (HALF // 2) + chip_of * cut
-        return pl.ds(pl.multiple_of(start, 16), cut)
-
-    far = chips // 2
+    far = max(1, chips // 2)
+    pair = min(2, chips)
+    at_z = lax.rem(chip, far) * pair + chip // far
+
+    def core_rows(core_of, k):
+        start, size = CHUNKS[k]
+        return pl.ds(pl.multiple_of(start + core_of * (size // 2), 16), size // 2)
+
+    def plane_rows(plane_of, k):
+        start, size = CHUNKS[k]
+        start = start + core * (size // 2) + plane_of * (size // 4)
+        return pl.ds(pl.multiple_of(start, 16), size // 4)
+
+    def cut_rows(plane_of, k, first_cut, count):
+        start, size = CHUNKS[k]
+        cut = size // 4 // chips
+        start = start + core * (size // 2) + plane_of * (size // 4) + first_cut * cut
+        return pl.ds(pl.multiple_of(start, 16), count * cut)
+
+    def pair_rows(plane_of, k):
+        return cut_rows(plane_of, k, lax.rem(chip, far) * pair, pair)
+
+    def early_copy(number, rows, send, recv, seg_to, lon_to, ref=None):
+        ref = packs.at[number] if ref is None else ref
+        return pltpu.make_async_remote_copy(
+            ref.at[rows], packs.at[number, rows], send, recv,
+            device_id=(seg_to, lon_to), device_id_type=MESH,
+        )
 
     def cut_copy(n, k):
-        of = lax.rem(chip + k * far, chips)
         if n < 4:
-            seg_to, lon_to, rows = seg + 2 * n, me, cut_rows(plane, of)
+            seg_to, lon_to, rows = seg + 2 * n, me, pair_rows(plane, k)
         else:
-            seg_to, lon_to, rows = facing + 2 * n, across, cut_rows(1 - plane, of)
+            seg_to, lon_to, rows = facing + 2 * n, across, pair_rows(1 - plane, k)
+        recv = a_recv.at[2 * jnp.minimum(seg, EARLY - 1) + k]
         ref = other.at[0] if n % 2 else packs.at[seg]
-        return pltpu.make_async_remote_copy(
-            ref.at[rows], packs.at[seg, rows], a_send.at[n, k], a_recv.at[jnp.minimum(seg, EARLY - 1)],
-            device_id=(lax.rem(seg_to, SEGS), lon_to), device_id_type=MESH,
-        )
+        return early_copy(seg, rows, a_send.at[n, k], recv, lax.rem(seg_to, SEGS), lon_to, ref)
 
     def send_cuts():
-        for n in (4, 1, 3, 5, 7, 2, 6):
-            for k in range(2 if chips > 1 else 1):
+        for k in range(2):
+            for n in (4, 1, 3, 5, 7, 2, 6):
                 cut_copy(n, k).start()
 
-    peers = [n for k in range(1, far) for n in (k, chips - k)]
-
-    def spread_copy(number, n):
-        rows = cut_rows(plane, chip)
-        return pltpu.make_async_remote_copy(
-            packs.at[number, rows], packs.at[number, rows], b_send.at[number, n], b_recv.at[number],
-            device_id=(seg, on_chip(n)), device_id_type=MESH,
-        )
-
-    def spread(number):
+    peers = [n for m in range(1, chips // 2) for n in (m, chips - m)]
+
+    def spread_copy(number, k, n):
+        at = 2 * number + k
+        rows = cut_rows(plane, k, at_z, 1)
+        return early_copy(number, rows, b_send.at[at, n], b_recv.at[at], seg, on_chip(n))
+
+    def spread(number, k):
         @pl.when(seg != number)
         def _():
-            rows = pl.ds(pl.multiple_of(core * HALF, 16), cut * (2 if chips > 1 else 1))
-            pltpu.make_async_remote_copy(
-                packs.at[number, rows], packs.at[number, rows], a_send.at[0, 0], a_recv.at[number],
-                device_id=(seg, across), device_id_type=MESH,
-            ).wait_recv()
+            at = 2 * number + k
+            rows = pair_rows(plane, k)
+            early_copy(number, rows, a_send.at[0, 0], a_recv.at[at], seg, across).wait_recv()
             for n in peers:
-                spread_copy(number, n).start()
-
-    def cross(number):
+                spread_copy(number, k, n).start()
+
+    def plane_copy(number, k, plane_of):
+        at = 2 * number + k
+        rows = plane_rows(plane_of, k)
+        return early_copy(number, rows, e_send.at[at], e_recv.at[at], seg, across)
+
+    def cross(number, k):
         @pl.when(seg != number)
         def _():
-            start = core * HALF + plane * (HALF // 2)
-            rows = pl.ds(pl.multiple_of(start, 16), max(1, len(peers)) * cut)
-            if chips > 1:
-                pltpu.make_async_remote_copy(
-                    packs.at[number, rows], packs.at[number, rows], b_send.at[number, 0],
-                    b_recv.at[number], device_id=(seg, across), device_id_type=MESH,
-                ).wait_recv()
-            cross_copy(number, plane).start()
-
-    def pair_up(number):
+            if peers:
+                at = 2 * number + k
+                rows = cut_rows(plane, k, 0, len(peers))
+                early_copy(number, rows, a_send.at[0, 0], b_recv.at[at], seg, across).wait_recv()
+            plane_copy(number, k, plane).start()
+
+    def core_copy(number, k, core_of):
+        at = 2 * number + k
+        rows = core_rows(core_of, k)
+        return early_copy(number, rows, d_send.at[at], d_recv.at[at], seg, sibling)
+
+    def pair_up(number, k):
         @pl.when(seg != number)
         def _():
-            cross_copy(number, 1 - plane).wait_recv()
-            sibling_copy(number, core).start()
+            plane_copy(number, k, 1 - plane).wait_recv()
+            core_copy(number, k, core).start()
 
     def halo_copy(number, way):
         return pltpu.make_async_remote_copy(
-            hist.at[number, pl.ds(TOK, TOK)],
-            hist.at[number, pl.ds(2 * TOK if way == 0 else 0, TOK)],
+            hist.at[number, pl.ds(BAND, BAND)],
+            hist.at[number, pl.ds(2 * BAND if way == 0 else 0, BAND)],
             h_send.at[number, way],
             h_recv.at[number, way],
             device_id=(seg, west if way == 0 else east),
@@ -383,7 +436,7 @@
         )
 
     swap_copy = pltpu.make_async_remote_copy(
-        swap, hist.at[0, pl.ds(TOK, TOK)], swap_sem.at[0], swap_sem.at[1],
+        swap, hist.at[0, pl.ds(BAND, BAND)], swap_sem.at[0], swap_sem.at[1],
         device_id=(seg, place), device_id_type=MESH,
     )
 
@@ -410,13 +463,13 @@
 
     @pl.when(folded)
     def _():
-        swap[...] = stage[...].astype(BF)
+        swap[...] = folded_band(stage[...])
         swap_copy.start()
         swap_copy.wait_recv()
 
     @pl.when(jnp.logical_not(folded))
     def _():
-        hist[0, TOK : 2 * TOK] = stage[...].astype(BF)
+        hist[0, BAND : 2 * BAND] = folded_band(stage[...])
 
     for way in range(2):
         halo_copy(0, way).start()
@@ -433,13 +486,19 @@
                 hit, 1.0, 0.0
             ).astype(BF)
     lon_ref[...] = lax.rem(token, LON).astype(F32)
-    spread(0)
+    spread(0, 0)
+    spread(0, 1)
+    cross(0, 0)
+    spread(1, 0)
+    cross(0, 1)
+    spread(1, 1)
+    pair_up(0, 0)
+    cross(1, 0)
+    pair_up(0, 1)
+    spread(2, 0)
     prepare(1)
-    cross(0)
-    spread(1)
-    cross(1)
-    spread(2)
-    pair_up(0)
+    cross(1, 1)
+    spread(2, 1)
 
     def params(number):
         return packs[number, PARAMS : PARAMS + 16, :].astype(F32)
@@ -452,75 +511,106 @@
         if not decoder:
             @pl.when(number == 0)
             def _():
-                @pl.when(seg >= SEGS // 2)
+                @pl.when((seg >= 0) & (seg < 8))
                 def _():
                     send_weights(1)
 
             @pl.when(number == 1)
             def _():
-                pair_up(1)
-                for n in range(EARLY, 7):
-                    first(n)
-                cross(2)
+                pair_up(1, 0)
+                pair_up(1, 1)
+                cross(2, 0)
+                cross(2, 1)
+                spread(3, 0)
+                spread(3, 1)
 
             @pl.when(number == 2)
             def _():
-                @pl.when(seg < SEGS // 2)
-                def _():
-                    send_weights(1)
-
-                pair_up(2)
-                for n in range(EARLY, 6):
-                    second(n)
+                pair_up(2, 0)
+                pair_up(2, 1)
+                cross(3, 0)
+                cross(3, 1)
+                first(4)
+                first(5)
 
             @pl.when(number == 3)
             def _():
-                third(3)
+                pair_up(3, 0)
+                pair_up(3, 1)
+                second(4)
+                second(5)
+                first(6)
+                first(7)
+
+            @pl.when(number == 4)
+            def _():
                 third(4)
-
-        @pl.when((number >= 2) & (number < SECTIONS - 5))
-        def _():
-            first(number + 5)
-
-        @pl.when((number >= 3) & (number < SECTIONS - 3))
-        def _():
-            second(number + 3)
-
-        @pl.when((number >= 4) & (number < SECTIONS - 1))
+                second(6)
+
+            @pl.when(number == 5)
+            def _():
+                third(5)
+                second(7)
+
+            @pl.when(number == 6)
+            def _():
+                third(6)
+                third(7)
+
+        @pl.when((number >= 7) & (number < SECTIONS - 1))
         def _():
             third(number + 1)
 
-        @pl.when(source(number) != seg)
+        @pl.when((number >= 6) & (number < SECTIONS - 2))
+        def _():
+            second(number + 2)
+
+        @pl.when((number >= 4) & (number < SECTIONS - 4))
+        def _():
+            first(number + 4)
+
+        def early(k):
+            for n in range(EARLY):
+                @pl.when((number == n) & (seg != n))
+                def _():
+                    core_copy(n, k, 1 - core).wait_recv()
+
+        @pl.when((source(number) != seg) & (number >= EARLY))
         def _():
             sibling_copy(number, 1 - core).wait_recv()
+
+        if not decoder:
+            early(0)
 
         tile = params(number)
         now = offset(tile)
         if decoder:
             before = offset(params(number - 1))
             earlier = now - offset(params(15 - number))
-            aside = dot(pick(token_ref[...], lon_ref[...], earlier), hist[16 - number])
+            aside = taken(pick(token_ref[...], lon_ref[...], earlier), hist, 16 - number)
         else:
             before = offset(params(jnp.maximum(number - 1, 0)))
             before = before * jnp.where(number > 0, 1.0, 0.0)
         chosen = pick(token_ref[...], lon_ref[...], now - before)
         for way in range(2):
             halo_copy(number, way).wait_recv()
-        u = dot(chosen, hist[number])
+        u = taken(chosen, hist, number)
         if decoder:
             u = ((u + aside) * 0.5).astype(BF).astype(F32)
         gain_a = side([tile[0:1] + tile[2:3] + tile[4:5], tile[1:2] + tile[3:4] + tile[5:6]])
         gain_b = side([tile[6:7] + tile[8:9] + tile[10:11], tile[7:8] + tile[9:10] + tile[11:12]])
 
         def strip(j):
-            start = STRIP * j if j < 9 else HALF + STRIP * (j - 9)
+            start = STRIP * j if j < 6 else AFTER + STRIP * (j - 6)
             return packs[number, start : start + STRIP, :]
 
         def bias(j):
-            start = HALF_W + TOK * j if j < 4 else HALF + HALF_W + TOK * (j - 4)
-            return packs[number, start : start + TOK, :]
-
-        hist[number + 1, TOK : 2 * TOK] = section(u, strip, bias, gain_a, gain_b)
+            return packs[number, BIAS + TOK * j : BIAS + TOK * j + TOK, :]
+
+        made = section(
+            u, strip, bias, gain_a, gain_b, None if decoder else functools.partial(early, 1)
+        )
+        hist[number + 1, BAND : 2 * BAND] = folded_band(made)
         for way in range(2):
             halo_copy(number + 1, way).start()
 
@@ -533,7 +623,7 @@
     back = pick(token.astype(F32), lon.astype(F32), -offset(params(SECTIONS - 1)))
     for way in range(2):
         halo_copy(SECTIONS, way).wait_recv()
-    final = dot(back, hist[SECTIONS]).astype(BF)
+    final = taken(back, hist, SECTIONS).astype(BF)
     final = side([final[ROWS * g : ROWS * g + ROWS] for g in range(3)])
     final = dot(final, share_ref[...]).astype(BF)
     for s in range(SEGS):
@@ -574,16 +664,18 @@
 
     @pl.when(seg < EARLY)
     def _():
-        for n in range(1, SEGS):
-            for k in range(2 if chips > 1 else 1):
+        for k in range(2):
+            for n in range(1, SEGS):
                 cut_copy(n, k).wait_send()
 
     def early_sent(number, carry):
         @pl.when(seg != number)
         def _():
-            for n in peers:
-                spread_copy(number, n).wait_send()
-            cross_copy(number, plane).wait_send()
+            for k in range(2):
+                for n in peers:
+                    spread_copy(number, k, n).wait_send()
+                plane_copy(number, k, plane).wait_send()
+                core_copy(number, k, core).wait_send()
 
         return carry
 
@@ -608,7 +700,7 @@
         swap_copy.wait_send()
 
     def finish(number, carry):
-        @pl.when((number < SECTIONS) & (source(number) != seg))
+        @pl.when((number >= EARLY) & (number < SECTIONS) & (source(number) != seg))
         def _():
             sibling_copy(number, core).wait_send()
 
@@ -664,16 +756,18 @@
         scratch_shapes=[pltpu.VMEM(a.shape, a.dtype) for a in stored] + [
             pltpu.VMEM((SECTIONS, PACK, 128), BF),
             pltpu.VMEM((2, PACK, 128), BF),
-            pltpu.VMEM((SECTIONS + 1, 3 * TOK, 256), BF),
+            pltpu.VMEM((SECTIONS + 1, 3 * BAND, 128), BF),
             pltpu.VMEM((TOK, 128), F32),
             pltpu.VMEM((TOK, 128), F32),
             pltpu.VMEM((768, 1024), BF),
             pltpu.VMEM((TOK, 256), F32),
-            pltpu.VMEM((TOK, 256), BF),
+            pltpu.VMEM((BAND, 128), BF),
             pltpu.VMEM((8, 256), F32),
             pltpu.VMEM((SEGS, ROWS, 128), BF),
             pltpu.VMEM((SEGS, ROWS, 128), BF),
-            dma((1,)), dma((2,)), dma((SEGS, 2)), dma((EARLY,)), dma((EARLY, 8)), dma((EARLY,)),
+            dma((1,)), dma((2,)), dma((SEGS, 2)), dma((2 * EARLY,)), dma((2 * EARLY, 8)),
+            dma((2 * EARLY,)), dma((2 * EARLY,)), dma((2 * EARLY,)), dma((2 * EARLY,)),
+            dma((2 * EARLY,)),
             dma((SECTIONS,)), dma((SECTIONS,)), dma((SECTIONS,)), dma((SECTIONS,)), dma((2, 4)),
             dma((SECTIONS,)), dma((SECTIONS,)), dma((SECTIONS,)), dma((SECTIONS + 1, 2)), dma((SECTIONS + 1, 2)), dma((SEGS,)),
             dma((SEGS,)), dma((6, 2)),

time: 146 us -> 142 us (0.973)
  the two profiles are of different devices: /device:TPU:4 before, /device:TPU:3 now
where the time goes in v5:
time: 142 us
  Pallas kernels  140 us (99%)
  local copies, waits for them, and re-layouts  1.88 us (1%)
    pallas_call x1, Pallas kernels, per_device(): pl.pallas_call(kernel, out_shape=jax.ShapeDtypeStruct((4, 2, TOK, 128), B...  140 us

profile of v5, /device:TPU:3, one launch (start us, length us, event | category | flops | bytes accessed | tf_op | source)
XLA Modules:
  0.0 142.2 jit_solution(12495889051401441326)
XLA Ops:
  0.0 140.3 %sections.1 = bf16[4,2,144,128]{3,2,1,0:T(8,128)(2,1)} custom-call(s32[4]{0:T(128)} %order_ref.1, s32[2,1,4]{2,1,0:T(1,128)} %bitcast.22, f32[2,2,192]{2,1,0:T(2,128)} %bitcast.21, bf16[4,12,12,2,192]{4,3,2,1,0:T(2,128)(2,1)} %bitcast.16, bf16[2,192,576]{2,1,0:T(8,128)(2,1)} %bitcast.19, bf16[2,192,192]{2,1,0:T(8,128)(2,1)} %bitcast.20, ...), custom_call_target="tpu_custom_call" | custom-call | tf_op jit(solution)/shard_map/sections/pallas_call | solution.py:751
  140.3 1.9 %copy.11 = bf16[4,2,12,12,24]{4,1,3,2,0:T(2,128)(2,1)} copy(bf16[4,2,12,12,24]{4,1,3,2,0:T(2,128)(2,1)} %bitcast.15) | data formatting | bytes 110592

commit v6 on v5

--- a/solution.py
+++ b/solution.py
@@ -523,6 +523,7 @@
                 cross(2, 1)
                 spread(3, 0)
                 spread(3, 1)
+                first(4)
 
             @pl.when(number == 2)
             def _():
@@ -530,14 +531,13 @@
                 pair_up(2, 1)
                 cross(3, 0)
                 cross(3, 1)
-                first(4)
+                second(4)
                 first(5)
 
             @pl.when(number == 3)
             def _():
                 pair_up(3, 0)
                 pair_up(3, 1)
-                second(4)
                 second(5)
                 first(6)
                 first(7)
@@ -545,16 +545,16 @@
             @pl.when(number == 4)
             def _():
                 third(4)
+                third(5)
                 second(6)
 
             @pl.when(number == 5)
             def _():
-                third(5)
+                third(6)
                 second(7)
 
             @pl.when(number == 6)
             def _():
-                third(6)
                 third(7)
 
         @pl.when((number >= 7) & (number < SECTIONS - 1))

time: 142 us -> 140 us (0.986)
  the two profiles are of different devices: /device:TPU:3 before, /device:TPU:4 now
where the time goes in v6:
time: 140 us; the launch traced here: 139 us
  Pallas kernels  137 us (98%)
  local copies, waits for them, and re-layouts  1.88 us (1%)
    pallas_call x1, Pallas kernels, per_device(): pl.pallas_call(kernel, out_shape=jax.ShapeDtypeStruct((4, 2, TOK, 128), B...  137 us

profile of v6, /device:TPU:4, one launch (start us, length us, event | category | flops | bytes accessed | tf_op | source)
XLA Modules:
  0.0 138.7 jit_solution(10308398894579610534)
XLA Ops:
  0.0 136.8 %sections.1 = bf16[4,2,144,128]{3,2,1,0:T(8,128)(2,1)} custom-call(s32[4]{0:T(128)} %order_ref.1, s32[2,1,4]{2,1,0:T(1,128)} %bitcast.22, f32[2,2,192]{2,1,0:T(2,128)} %bitcast.21, bf16[4,12,12,2,192]{4,3,2,1,0:T(2,128)(2,1)} %bitcast.16, bf16[2,192,576]{2,1,0:T(8,128)(2,1)} %bitcast.19, bf16[2,192,192]{2,1,0:T(8,128)(2,1)} %bitcast.20, ...), custom_call_target="tpu_custom_call" | custom-call | tf_op jit(solution)/shard_map/sections/pallas_call | solution.py:751
  136.9 1.9 %copy.11 = bf16[4,2,12,12,24]{4,1,3,2,0:T(2,128)(2,1)} copy(bf16[4,2,12,12,24]{4,1,3,2,0:T(2,128)(2,1)} %bitcast.15) | data formatting | bytes 110592

commit v7 on v6

--- a/solution.py
+++ b/solution.py
@@ -194,7 +194,8 @@
     def on_chip(n):
         return plane * half_ring + 2 * lax.rem(chip + n, chips) + core
 
-    for n in range(1, chips):
+    peers = [n for m in range(1, chips // 2) for n in (m, chips - m)]
+    for n in peers:
         greet(seg, on_chip(n))
     greet(seg, across)
     for n in range(1, 4):
@@ -284,9 +285,9 @@
         )
 
     def send_weights(half):
+        for n in (2, 1, 3):
+            own_copy(half, n).start()
         facing_copy(own_number(half)).start()
-        for n in (1, 3, 2):
-            own_copy(half, n).start()
 
     def facing_copy(number):
         rows = part_rows(plane)
@@ -384,8 +385,6 @@
             for n in (4, 1, 3, 5, 7, 2, 6):
                 cut_copy(n, k).start()
 
-    peers = [n for m in range(1, chips // 2) for n in (m, chips - m)]
-
     def spread_copy(number, k, n):
         at = 2 * number + k
         rows = cut_rows(plane, k, at_z, 1)
@@ -450,7 +449,7 @@
             start = 72 * level + LON * n
             stage[start : start + LON, :WIDTH] = cells[:, level, :]
 
-    pl.semaphore_wait(barrier, 14 + chips + 3)
+    pl.semaphore_wait(barrier, 18 + len(peers))
 
     @pl.when(seg < EARLY)
     def _():
@@ -533,13 +532,13 @@
                 cross(3, 1)
                 second(4)
                 first(5)
+                first(6)
 
             @pl.when(number == 3)
             def _():
                 pair_up(3, 0)
                 pair_up(3, 1)
                 second(5)
-                first(6)
                 first(7)
 
             @pl.when(number == 4)
@@ -570,10 +569,9 @@
             first(number + 4)
 
         def early(k):
-            for n in range(EARLY):
-                @pl.when((number == n) & (seg != n))
-                def _():
-                    core_copy(n, k, 1 - core).wait_recv()
+            @pl.when((number < EARLY) & (seg != number))
+            def _():
+                core_copy(number, k, 1 - core).wait_recv()
 
         @pl.when((source(number) != seg) & (number >= EARLY))
         def _():

time: 140 us -> 140 us (level)
  no operation moved by 1% of the time
where the time goes in v7:
time: 140 us; the launch traced here: 139 us
  Pallas kernels  137 us (98%)
  local copies, waits for them, and re-layouts  1.88 us (1%)
    pallas_call x1, Pallas kernels, per_device(): pl.pallas_call(kernel, out_shape=jax.ShapeDtypeStruct((4, 2, TOK, 128), B...  137 us

profile of v7, /device:TPU:4, one launch (start us, length us, event | category | flops | bytes accessed | tf_op | source)
XLA Modules:
  0.0 139.0 jit_solution(11700027200915777011)
XLA Ops:
  0.0 137.1 %sections.1 = bf16[4,2,144,128]{3,2,1,0:T(8,128)(2,1)} custom-call(s32[4]{0:T(128)} %order_ref.1, s32[2,1,4]{2,1,0:T(1,128)} %bitcast.22, f32[2,2,192]{2,1,0:T(2,128)} %bitcast.21, bf16[4,12,12,2,192]{4,3,2,1,0:T(2,128)(2,1)} %bitcast.16, bf16[2,192,576]{2,1,0:T(8,128)(2,1)} %bitcast.19, bf16[2,192,192]{2,1,0:T(8,128)(2,1)} %bitcast.20, ...), custom_call_target="tpu_custom_call" | custom-call | tf_op jit(solution)/shard_map/sections/pallas_call | solution.py:749
  137.1 1.9 %copy.11 = bf16[4,2,12,12,24]{4,1,3,2,0:T(2,128)(2,1)} copy(bf16[4,2,12,12,24]{4,1,3,2,0:T(2,128)(2,1)} %bitcast.15) | data formatting | bytes 110592
